TPU v7x, 256 devices: a whole 4x4x8 slice. The times are simulated.
256 devices in a mesh: dp: 32 (over z, y), expert: 8 (over x, core).
Axes of the slice: x: 4, y: 4, z: 8, core: 2. Of those that a mesh axis runs over, the one named last changes fastest.
Arguments:
- residual: bfloat16 [32768, 4096], P(('dp', 'expert')), may hold values from -36 to 36
- norm_gain: float32 [4096], replicated, may hold values from 0.5 to 1.5
- router_weight: bfloat16 [16, 4096], replicated, may hold values from -8 to 8
- up_weight: bfloat16 [4096, 16, 768], P('dp', 'expert'), may hold values from -0.09375 to 0.09375
- routes: int32 [32768, 2], P(('dp', 'expert')), may hold values from 0 to 15, all different within a row; in each aligned block of 128 rows (0 to 127, 128 to 255, ...) at most 20 rows name the same one
- keep_flags: int32 [32768, 2], P(('dp', 'expert')), may hold values 0 or 1
- gate_grad: float32 [32768, 2], P(('dp', 'expert')), may hold values from -24 to 24
- grad_hidden: bfloat16 [16, 5120, 768], P('expert', 'dp'), may hold values from -6 to 6
Outputs:
- resid_grad: bfloat16 [32768, 4096], P(('dp', 'expert'))
- up_grad: float32 [4096, 16, 768], P('dp', 'expert')
- router_grad: float32 [16, 4096], replicated
- gain_grad: float32 [4096], replicated
Inputs may be any that keep to these rules, and one draw needn't show every extreme that they name: `routes`: within the 128 tokens of one device (aligned blocks of rows) no expert is named by more than 20 choices, and in every draw some expert is named by exactly 20; a token's two experts differ.
All inputs are finite; a program needn't handle non-finite values. No bound on the sum of `keep_flags` on one device may be relied on, other than what follows from the above.
Results may differ from a plain program's by a relative error of at most 0.02.
The roundings to bfloat16 on the way count: a program that leaves them out, or rounds other values in their place, can miss the bound.
Values may be sent and summed in bfloat16 or wider, within the bound.
A program may use at most 128 MiB of HBM per device.

v0:
```python
import jax
import jax.numpy as jnp
from jax import lax
from jax.sharding import PartitionSpec as P


def silu_slope(preact):
    sigmoid_value = jax.nn.sigmoid(preact)
    return sigmoid_value * (1.0 + preact * (1.0 - sigmoid_value))


def expert_backward(slots_in, full_weight, hidden_grad):
    preact = jnp.einsum("esd,def->esf", slots_in, full_weight, preferred_element_type=jnp.float32)
    pre_grad = (hidden_grad.astype(jnp.float32) * silu_slope(preact)).astype(jnp.bfloat16)
    back_rows = jnp.einsum(
        "esf,def->esd", pre_grad, full_weight, preferred_element_type=jnp.float32
    )
    return (pre_grad, back_rows.astype(jnp.bfloat16))


def tile_maker(slots_in, pre_grad):
    return jnp.einsum("esd,esf->def", slots_in, pre_grad, preferred_element_type=jnp.float32)


def local(
    residual, norm_gain, router_weight, up_weight, routes, keep_flags, gate_grad, grad_hidden
):
    row_count = residual.shape[0]
    model_width = residual.shape[1]
    top_count = routes.shape[1]
    owner_count = lax.axis_size("expert")
    local_experts = up_weight.shape[1]
    expert_count = local_experts * owner_count
    capacity = grad_hidden.shape[1] // owner_count
    slot_total = expert_count * capacity
    wide_rows = residual.astype(jnp.float32)
    inv_rms = lax.rsqrt(jnp.mean(wide_rows * wide_rows, axis=1, keepdims=True) + 1e-06)
    normed = (wide_rows * inv_rms * norm_gain[None, :]).astype(jnp.bfloat16)
    expert_ids = jnp.arange(expert_count, dtype=jnp.int32)
    flat_routes = routes.reshape(-1)
    member = (flat_routes[:, None] == expert_ids[None, :]).astype(jnp.int32)
    ahead = jnp.cumsum(member, axis=0) - member
    position = jnp.sum(ahead * member, axis=1)
    target = (
        flat_routes % local_experts * (owner_count * capacity)
        + flat_routes // local_experts * capacity
        + position
    )
    target = jnp.where(keep_flags.reshape(-1) == 1, target, slot_total)
    slot_ids = jnp.arange(slot_total, dtype=jnp.int32)
    placed = jnp.any(
        target.reshape(row_count, top_count)[:, :, None] == slot_ids[None, None, :], axis=1
    ).astype(jnp.bfloat16)
    logits = jnp.einsum("td,ed->te", normed, router_weight, preferred_element_type=jnp.float32)
    probs = jax.nn.softmax(logits, axis=1)
    choose = (routes[:, :, None] == expert_ids[None, None, :]).astype(jnp.float32)
    weighted = keep_flags.astype(jnp.float32) * gate_grad
    prob_grad = jnp.sum(choose * weighted[:, :, None], axis=1)
    logit_grad = (probs * (prob_grad - jnp.sum(probs * prob_grad, axis=1, keepdims=True))).astype(
        jnp.bfloat16
    )
    router_part = jnp.einsum("te,td->ed", logit_grad, normed, preferred_element_type=jnp.float32)
    router_back = jnp.einsum(
        "te,ed->td", logit_grad, router_weight, preferred_element_type=jnp.float32
    )
    sending = jnp.einsum("ts,td->sd", placed, normed, preferred_element_type=jnp.float32).astype(
        jnp.bfloat16
    )
    sending = sending.reshape(local_experts, owner_count, capacity, model_width)
    arrived = lax.all_to_all(sending, "expert", split_axis=1, concat_axis=1, tiled=True)
    slots_in = arrived.reshape(local_experts, owner_count * capacity, model_width)
    full_weight = lax.all_gather(up_weight, "dp", axis=0, tiled=True)
    pre_grad, back_rows = expert_backward(slots_in, full_weight, grad_hidden)
    up_grad = lax.psum_scatter(
        tile_maker(slots_in, pre_grad).astype(jnp.bfloat16), "dp", scatter_dimension=0, tiled=True
    ).astype(jnp.float32)
    leaving = back_rows.reshape(local_experts, owner_count, capacity, model_width)
    returned = lax.all_to_all(leaving, "expert", split_axis=1, concat_axis=1, tiled=True).reshape(
        slot_total, model_width
    )
    from_experts = jnp.einsum("ts,sd->td", placed, returned, preferred_element_type=jnp.float32)
    total_grad = from_experts + router_back
    gain_part = jnp.sum(total_grad * wide_rows * inv_rms, axis=0)
    scaled = total_grad * norm_gain[None, :]
    inner = jnp.mean(scaled * wide_rows, axis=1, keepdims=True)
    resid_grad = (inv_rms * scaled - wide_rows * inv_rms * inv_rms * inv_rms * inner).astype(
        jnp.bfloat16
    )
    router_grad, gain_grad = lax.psum((router_part, gain_part), ("dp", "expert"))
    return (resid_grad, up_grad, router_grad, gain_grad)


def solution(mesh):
    in_specs = (
        P(("dp", "expert"), None),
        P(),
        P(),
        P("dp", "expert", None),
        P(("dp", "expert"), None),
        P(("dp", "expert"), None),
        P(("dp", "expert"), None),
        P("expert", "dp", None),
    )
    out_specs = (P(("dp", "expert"), None), P("dp", "expert", None), P(), P())
    return jax.shard_map(local, mesh=mesh, in_specs=in_specs, out_specs=out_specs, check_vma=False)
```

profile of v0, /device:TPU:1, one launch (start us, length us, event | category | flops | bytes accessed | tf_op | source)
XLA Modules:
  0.0 458.1 jit_solution(7782347563246981455)
XLA Ops:
  8.1 1.9 copy.73
  10.0 0.8 copy.61
  11.1 0.7 broadcast_compare_fusion.1
  11.9 0.6 reduce-window.6
  13.0 0.7 broadcast_compare_fusion
  14.0 0.3 fusion.10
  14.3 2.1 convolution_convert_fusion.2
  16.5 2.4 reshape.95
  18.8 4.6 %copy.72 = bf16[2,8,20,4096]{3,0,2,1:T(2,128)(2,1)S(1)} copy(bf16[2,8,20,4096]{3,2,1,0:T(8,128)(2,1)} %reshape.95) | data formatting | bytes 5242880 | tf_op jit(solution)/shard_map/reshape | solution.py:69
  23.5 37.9 %all_to_all.10 = bf16[2,8,20,4096]{3,0,2,1:T(2,128)(2,1)S(1)} all-to-all(bf16[2,8,20,4096]{3,0,2,1:T(2,128)(2,1)S(1)} %copy.72), channel_id=1, replica_groups=mesh['dp'=32,'expert'=8] {'expert'}, dimensions={1} | all-to-all | bytes 5242880 | tf_op jit(solution)/shard_map/all_to_all | solution.py:70
  61.3 73.8 %all-gather.2.cloned.1.call-done = bf16[4096,2,768]{2,0,1:T(8,128)(2,1)} async-done(((bf16[128,2,768]{2,0,1:T(8,128)(2,1)}), bf16[4096,2,768]{2,0,1:T(8,128)(2,1)}) %all-gather.2.cloned.1.call-update) | async-done | bytes 12582928 | tf_op jit(solution)/shard_map/all_gather | solution.py:72
  135.2 9.2 %fusion.3 = f32[2,160,768]{2,1,0:T(8,128)S(1)} fusion(bf16[4096,2,768]{2,0,1:T(8,128)(2,1)} %all-gather.2.cloned.1.call-done, bf16[2,160,4096]{2,0,1:T(2,128)(2,1)S(1)} %bitcast.37), kind=kOutput, calls=%fused_computation.11 | convolution fusion | flops 2013265920 | bytes 16187392 | tf_op jit(solution)/shard_map/esd,def->esf/dot_general | solution.py:13
  144.4 7.2 %convolution_convert_fusion = bf16[2,768,4096]{2,1,0:T(8,128)(2,1)} fusion(bf16[2,160,4096]{2,0,1:T(2,128)(2,1)S(1)} %bitcast.38, f32[2,160,768]{2,1,0:T(8,128)S(1)} %fusion.3, bf16[2,160,768]{2,1,0:T(8,128)(2,1)S(1)} %copy-done.7), kind=kOutput, calls=%fused_computation | convolution fusion | flops 2022014976 | bytes 16678912 | tf_op jit(solution)/shard_map/esd,esf->def/dot_general | solution.py:22
  151.6 16.6 %copy.81 = bf16[4096,1536]{1,0:T(8,128)(2,1)} copy(bf16[4096,1536]{0,1:T(8,128)(2,1)} %bitcast.35) | data formatting | bytes 25165824
  168.2 1.2 copy-done.9
  169.4 8.8 %convolution_convert_fusion.1 = bf16[2,160,4096]{2,1,0:T(8,128)(2,1)S(1)} fusion(bf16[4096,2,768]{2,0,1:T(8,128)(2,1)} %all-gather.2.cloned.1.call-done, f32[2,160,768]{2,1,0:T(8,128)S(1)} %copy-done.9, bf16[2,160,768]{2,1,0:T(8,128)(2,1)S(1)} %copy-done.7), kind=kOutput, calls=%fused_computation.1 | convolution fusion | flops 2017034240 | bytes 16678912 | tf_op jit(solution)/shard_map/esf,def->esd/dot_general | solution.py:15
  178.2 4.2 copy.75
  182.5 5.4 %all-to-all-start.1 = ((bf16[2,8,20,4096]{3,0,2,1:T(2,128)(2,1)}), bf16[2,8,20,4096]{3,0,2,1:T(2,128)(2,1)}, u32[]{:S(2)}, u32[]{:S(2)}) async-start(bf16[2,8,20,4096]{3,0,2,1:T(2,128)(2,1)} %bitcast.36), calls=%async_computation.1 | async-start | bytes 5242880 | tf_op jit(solution)/shard_map/all_to_all | solution.py:78
  187.9 0.5 fusion.41
  188.5 1.1 fusion.36
  189.7 30.4 %all-to-all-done.1 = bf16[2,8,20,4096]{3,0,2,1:T(2,128)(2,1)} async-done(((bf16[2,8,20,4096]{3,0,2,1:T(2,128)(2,1)}), bf16[2,8,20,4096]{3,0,2,1:T(2,128)(2,1)}, u32[]{:S(2)}, u32[]{:S(2)}) %all-to-all-start.1) | async-done | bytes 2621472 | tf_op jit(solution)/shard_map/all_to_all | solution.py:78
  220.1 5.4 %copy.76 = bf16[2,8,20,4096]{3,2,1,0:T(8,128)(2,1)} copy(bf16[2,8,20,4096]{3,0,2,1:T(2,128)(2,1)} %all-to-all-done.1) | data formatting | bytes 5242880 | tf_op jit(solution)/shard_map/all_to_all | solution.py:78
  225.5 4.3 reshape.98
  229.8 2.5 fusion.42
  232.4 0.9 fusion.13
  233.3 1.7 fusion.9
  234.9 74.4 %psum.15 = f32[4096]{0:T(1024)} all-reduce(f32[4096]{0:T(1024)S(1)} %get-tuple-element.20), channel_id=1, replica_groups=mesh['dp'=32,'expert'=8] {'dp','expert'}, use_global_device_ids=true, to_apply=%region_13.14 | all-reduce | flops 4096 | bytes 32768 | tf_op jit(solution)/shard_map/psum | solution.py:89
  309.3 90.1 %reduce-scatter.4.cloned.1.call-done = bf16[128,1536]{1,0:T(8,128)(2,1)} async-done(((bf16[4096,1536]{1,0:T(8,128)(2,1)}), bf16[128,1536]{1,0:T(8,128)(2,1)}) %reduce-scatter.4.cloned.1.call-update) | async-done | bytes 393232
  399.5 1.2 copy.82
  400.7 1.1 copy.78
  401.8 47.2 %all-reduce.2.cloned.1.call-done = f32[16,4096]{1,0:T(8,128)} async-done(((f32[16,4096]{1,0:T(8,128)}), f32[16,4096]{1,0:T(8,128)}) %all-reduce.2.cloned.1.call-update) | async-done | bytes 262160 | tf_op jit(solution)/shard_map/psum | solution.py:89
  448.9 1.7 copy.93
  (45 shorter events, 1.5 us)
Async XLA Ops:
  8.0 179.9 %copy-start = (bf16[16,4096]{1,0:T(8,128)(2,1)S(1)}, bf16[16,4096]{1,0:T(8,128)(2,1)}, u32[]{:S(2)}) copy-start(bf16[16,4096]{1,0:T(8,128)(2,1)} %param.10) | copy-start | bytes 393220
  8.0 6.0 %copy-start.1 = (bf16[128,4096]{1,0:T(8,128)(2,1)S(1)}, bf16[128,4096]{1,0:T(8,128)(2,1)}, u32[]{:S(2)}) copy-start(bf16[128,4096]{1,0:T(8,128)(2,1)} %param.8) | copy-start | bytes 3145732
  8.0 6.3 %copy-start.3 = (f32[4096]{0:T(1024)S(1)}, f32[4096]{0:T(1024)}, u32[]{:S(2)}) copy-start(f32[4096]{0:T(1024)} %param.9) | copy-start | bytes 49156
  8.0 127.2 %all-gather.2.cloned.1.call-start = ((), (), s32[]{:S(2)}) async-start(), calls=%async_computation.3 | async-start | bytes 12976128 | tf_op jit(solution)/shard_map/all_gather | solution.py:72
  10.0 389.5 %reduce-scatter.4.cloned.1.call-start = ((), (), s32[]{:S(2)}) async-start(), calls=%async_computation.5 | async-start | bytes 12976128
  135.2 9.2 %copy-start.7 = (bf16[2,160,768]{2,1,0:T(8,128)(2,1)S(1)}, bf16[2,160,768]{2,1,0:T(8,128)(2,1)}, u32[]{:S(2)}) copy-start(bf16[2,160,768]{2,1,0:T(8,128)(2,1)} %param.15) | copy-start | bytes 1474564
  144.4 7.2 %copy-start.8 = (f32[2,160,768]{2,1,0:T(8,128)}, f32[2,160,768]{2,1,0:T(8,128)S(1)}, u32[]{:S(2)}) copy-start(f32[2,160,768]{2,1,0:T(8,128)S(1)} %fusion.3) | copy-start | bytes 2949124
  168.2 1.2 copy-start.9
  182.5 5.5 %copy-start.2 = (bf16[128,4096]{1,0:T(8,128)(2,1)S(1)}, bf16[128,4096]{1,0:T(8,128)(2,1)}, u32[]{:S(2)}) copy-start(bf16[128,4096]{1,0:T(8,128)(2,1)} %param.8) | copy-start | bytes 3145732
  182.5 6.0 %copy-start.5 = (s32[128,2]{0,1:T(2,128)S(1)}, s32[128,2]{0,1:T(2,128)}, u32[]{:S(2)}) copy-start(s32[128,2]{0,1:T(2,128)} %param.13) | copy-start | bytes 3076
  182.5 6.0 %copy-start.6 = (f32[128,2]{0,1:T(2,128)S(1)}, f32[128,2]{0,1:T(2,128)}, u32[]{:S(2)}) copy-start(f32[128,2]{0,1:T(2,128)} %param.14) | copy-start | bytes 3076
  182.5 6.0 %copy-start.4 = (s32[128,2]{0,1:T(2,128)S(1)}, s32[128,2]{0,1:T(2,128)}, u32[]{:S(2)}) copy-start(s32[128,2]{0,1:T(2,128)} %param.12) | copy-start | bytes 3076
  182.5 37.6 %all-to-all-start.1 = ((bf16[2,8,20,4096]{3,0,2,1:T(2,128)(2,1)}), bf16[2,8,20,4096]{3,0,2,1:T(2,128)(2,1)}, u32[]{:S(2)}, u32[]{:S(2)}) async-start(bf16[2,8,20,4096]{3,0,2,1:T(2,128)(2,1)} %bitcast.36), calls=%async_computation.1 | async-start | bytes 5242880 | tf_op jit(solution)/shard_map/all_to_all | solution.py:78
  187.9 261.0 %all-reduce.2.cloned.1.call-start = ((), (), s32[]{:S(2)}) async-start(), calls=%async_computation.4 | async-start | bytes 524288 | tf_op jit(solution)/shard_map/psum | solution.py:89
Sparse Core Ops, SparseCore 0:
  12.0 123.1 all-gather.1
  168.3 231.0 reduce-scatter.3
Sparse Core Ops, SparseCore 1:
  194.4 254.5 all-reduce.1
where the time goes:
time: 460 us; the launch traced here: 458 us
  waiting for transfers between devices  242 us (53%)
  blocking collectives  112 us (24%)
  local copies, waits for them, and re-layouts  46.3 us (10%)
  matrix products  32.4 us (7%)
  between operations  15.7 us (3%)
  starting transfers between devices  5.52 us (1%)
    unnamed x4, waiting for transfers between devices  90.2 us
    psum x1, blocking collectives, local(): lax.psum((router_part, gain_part), ('dp', 'expert'))  74.4 us
    all_gather x1, waiting for transfers between devices, local(): full_weight = lax.all_gather(up_weight, 'dp', axis=0, tiled=True)  73.8 us
    psum x1, waiting for transfers between devices, local(): lax.psum((router_part, gain_part), ('dp', 'expert'))  47.2 us
    all_to_all x1, blocking collectives, local(): lax.all_to_all(sending, 'expert', split_axis=1, concat_axis=1, tiled=True)  37.9 us
    all_to_all x1, waiting for transfers between devices, local(): lax.all_to_all(leaving, 'expert', split_axis=1, concat_axis=1, tiled=True)  30.4 us
    unnamed x26, local copies, waits for them, and re-layouts  24.5 us
  transfers between devices with their start and end apart: 4, of which 4 were waited for; matrix products, arithmetic and copies ran while one was open for 10% of the time, Pallas kernels for 0%

commit v1 on v0

v1 whole, which is shorter than its diff:
```python
import functools

import jax
import jax.numpy as jnp
import numpy as np
from jax import lax
from jax.experimental import pallas as pl
from jax.experimental.pallas import tpu as pltpu
from jax.sharding import PartitionSpec as P

NY = 4
BF16 = jnp.bfloat16
F32 = jnp.float32


def nn(a, b):
    return lax.dot_general(a, b, (((1,), (0,)), ((), ())), preferred_element_type=F32)


def nt(a, b):
    return lax.dot_general(a, b, (((1,), (1,)), ((), ())), preferred_element_type=F32)


def tn(a, b):
    return lax.dot_general(a, b, (((0,), (0,)), ((), ())), preferred_element_type=F32)


def silu_slope(v):
    s = jax.nn.sigmoid(v)
    return s * (1.0 + v * (1.0 - s))


class Dims:
    def __init__(self, mesh, tokens, width, ff, cap):
        self.nz = mesh.shape["dp"] // NY
        self.nx = mesh.shape["expert"]
        self.t = tokens
        self.d = width
        self.cb = width // (self.nz * NY)
        self.q = width // NY
        self.ff = ff
        self.cap = cap
        self.e = 2 * self.nx
        self.rows = NY * cap
        self.m = self.nx * self.rows
        self.blk = self.nx * cap


def kernel(
    c,
    residual,
    norm_gain,
    router_weight,
    weight,
    routes,
    keep,
    gate,
    grad_hidden,
    order,
    order_t,
    resid_out,
    up_out,
    router_out,
    gain_out,
    inv_ref,
    tok_send,
    tok,
    info,
    rw_slices,
    place,
    slots_out,
    slots,
    wfull,
    part,
    part_perm,
    rs_a,
    rs_b,
    pre_grad,
    pg_rows,
    backs,
    returned,
    wg_out,
    wg_in,
    acc,
    tok_back,
    tok_ret,
    gain_acc,
    ar0,
    ar1,
    ar2,
    ar3,
    ar4,
    sem_tok,
    sem_info,
    sem_slot,
    sem_w,
    sem_rs,
    sem_pg,
    sem_back,
    sem_wg,
    sem_ret,
    sem_ar,
):
    nz, nx, t, q, cb, cap, rows, m, blk = c.nz, c.nx, c.t, c.q, c.cb, c.cap, c.rows, c.m, c.blk
    half = nz // 2
    hb = blk // 2
    hc = cb // 2
    dp = lax.axis_index("dp")
    me = lax.axis_index("expert")
    z, y = dp // NY, dp % NY

    def at_y(d):
        return (y + d) % NY

    def at_z(d):
        return (z + d + nz) % nz

    def at_x(d):
        return (me + d) % nx

    def to_y(d):
        return {"dp": z * NY + at_y(d)}

    def to_z(d):
        return {"dp": at_z(d) * NY + y}

    def to_x(d):
        return {"expert": at_x(d)}

    def remote(src, dst, sems, index, target):
        return pltpu.make_async_remote_copy(
            src_ref=src,
            dst_ref=dst,
            send_sem=sems.at[(0, *index)],
            recv_sem=sems.at[(1, *index)],
            device_id=target,
            device_id_type=pl.DeviceIdType.MESH,
        )

    barrier = pltpu.get_barrier_semaphore()
    for d in range(1, NY):
        pl.semaphore_signal(barrier, inc=1, device_id=to_y(d))
    for d in range(1, nz):
        pl.semaphore_signal(barrier, inc=1, device_id=to_z(d))
    for d in range(1, nx):
        pl.semaphore_signal(barrier, inc=1, device_id=to_x(d))
    pl.semaphore_wait(barrier, NY + nz + nx - 3)

    for i in range(2):
        wfull[i, z] = weight[i]

    def w_copy(i, way, s):
        sign = 1 if way == 0 else -1
        source = at_z(-sign * (s - 1))
        ref = wfull.at[i, source]
        if s == half:
            ref = ref.at[pl.ds(way * hc, hc)]
        return remote(ref, ref, sem_w, (i, way, s - 1), to_z(sign))

    def w_recv(i, way, s):
        sign = 1 if way == 0 else -1
        ref = wfull.at[i, at_z(-sign * s)]
        if s == half:
            ref = ref.at[pl.ds(way * hc, hc)]
        remote(ref, ref, sem_w, (i, way, s - 1), to_z(-sign)).wait_recv()

    def w_step(s):
        for i in range(2):
            for way in range(2):
                if s > 1:
                    w_recv(i, way, s - 1)
                if s <= half:
                    w_copy(i, way, s).start()

    w_step(1)

    sums = jnp.zeros((t, cb), F32)
    for b in range(nz * NY):
        x = residual[:, b * cb : (b + 1) * cb].astype(F32)
        sums = sums + x * x
    inv_rms = lax.rsqrt(jnp.sum(sums, axis=1, keepdims=True) * (1.0 / c.d) + 1e-06)
    inv_ref[...] = jnp.broadcast_to(inv_rms, inv_ref.shape)
    for b in range(nz * NY):
        span = slice(b * cb, (b + 1) * cb)
        inner = slice((b // NY) * cb, (b // NY + 1) * cb)
        x = residual[:, span].astype(F32)
        tok_send[b % NY, :, inner] = (x * inv_rms * norm_gain[:, span]).astype(BF16)
        rw_slices[b % NY, :, inner] = router_weight[:, span]

    def tok_copy(d):
        return remote(tok_send.at[at_y(d)], tok.at[y], sem_tok, (d - 1,), to_y(d))

    for d in (2, 1, 3):
        tok_copy(d).start()

    logits = jnp.zeros((c.e, t), F32)
    for p in range(NY):
        logits = logits + nt(rw_slices[p], tok_send[p])
    top = jnp.max(logits, axis=0, keepdims=True)
    expo = jnp.exp(logits - top)
    probs = expo / jnp.sum(expo, axis=0, keepdims=True)
    expert_ids = lax.broadcasted_iota(jnp.int32, (c.e, t), 0)
    members = [(expert_ids == routes[k : k + 1, :]) for k in range(2)]
    counts = sum(jnp.where(mk, 1.0, 0.0) for mk in members)
    before = lax.broadcasted_iota(jnp.int32, (t, t), 0) < lax.broadcasted_iota(jnp.int32, (t, t), 1)
    ahead = nn(counts.astype(BF16), jnp.where(before, 1.0, 0.0).astype(BF16))
    prob_grad = jnp.zeros((c.e, t), F32)
    info[y] = jnp.zeros_like(info[y])
    for k in range(2):
        kept = keep[k : k + 1, :]
        prob_grad = prob_grad + jnp.where(members[k], kept.astype(F32) * gate[k : k + 1, :], 0.0)
        slot = jnp.sum(jnp.where(members[k], ahead, 0.0), axis=0, keepdims=True)
        route = routes[k : k + 1, :]
        base = (route & 1) * m + (route >> 1) * rows + y * cap
        row = jnp.where(kept == 1, base.astype(F32) + slot, -1.0)
        info[y, c.e + k : c.e + k + 1, :] = row
    logit_grad = (probs * (prob_grad - jnp.sum(probs * prob_grad, axis=0, keepdims=True))).astype(BF16)
    info[y, 0 : c.e, :] = logit_grad.astype(F32)

    def info_copy(d):
        return remote(info.at[y], info.at[y], sem_info, (d - 1,), to_y(d))

    for d in (2, 1, 3):
        info_copy(d).start()
    tok[y] = tok_send[y]
    w_step(2)
    for d in range(1, NY):
        ref = info.at[at_y(-d)]
        remote(ref, ref, sem_info, (d - 1,), to_y(-d)).wait_recv()
    for d in range(1, NY):
        ref = tok.at[at_y(-d)]
        remote(ref, ref, sem_tok, (d - 1,), to_y(-d)).wait_recv()

    def slot_copy(i, d):
        return remote(slots_out.at[i, at_x(d)], slots.at[i, me], sem_slot, (i, d - 1), to_x(d))

    def make_slots(i):
        targets = [
            jnp.concatenate([info[j, c.e + k : c.e + k + 1, :] for j in range(NY)], axis=1)
            for k in range(2)
        ]
        tokens = tok[...].reshape(NY * t, q)

        def place_rows(owner):
            row = lax.broadcasted_iota(jnp.int32, (rows, NY * t), 0) + (i * m + owner * rows)
            row = row.astype(F32)
            hit = (row == targets[0]) | (row == targets[1])
            placed = jnp.where(hit, 1.0, 0.0).astype(BF16)
            place[i, owner] = placed
            return nn(placed, tokens).astype(BF16)

        def step(d, carry):
            slots_out[i, at_x(d)] = place_rows(at_x(d))
            slot_copy(i, d).start()
            return carry

        lax.fori_loop(1, nx, step, 0)
        slots[i, me] = place_rows(me)

    make_slots(0)
    w_step(3)
    make_slots(1)
    for s in range(4, half + 1):
        w_step(s)

    lg_all = jnp.concatenate([info[j, 0 : c.e, :] for j in range(NY)], axis=1).astype(BF16)
    tokens = tok[...].reshape(NY * t, q)
    ar0[0 : c.e, :] = nn(lg_all, tokens)
    gain_acc[...] = jnp.zeros_like(gain_acc)
    for j in range(NY):
        back = tn(info[j, 0 : c.e, :].astype(BF16), rw_slices[y]) * tok[j].astype(F32)
        gain_acc[...] += jnp.sum(back.reshape(t // 8, 8, q), axis=0)

    def rs_copy(i, way, s):
        sign = 1 if way == 0 else -1
        if s == 0:
            src = part_perm.at[i, at_y(2), pl.ds(way * hb, hb)]
            dst = rs_a.at[i, way]
        else:
            src = part_perm.at[i, at_y(sign + NY)]
            dst = rs_b.at[i, way]
        return remote(src, dst, sem_rs, (i, way, s), to_y(sign + NY))

    def permuted(i, j):
        return nn(order[pl.ds(pl.multiple_of(j * blk, 16), blk), :], part[i])

    def preact_part(i):
        for s in range(half, half + 1):
            for way in range(2):
                w_recv(i, way, s)

        def wait_slots(d, carry):
            ref = slots.at[i, at_x(nx - d)]
            remote(ref, ref, sem_slot, (i, d - 1), to_x(nx - d)).wait_recv()
            return carry

        lax.fori_loop(1, nx, wait_slots, 0)

        def step(h, carry):
            some = slots[i, pl.ds(2 * h, 2)].reshape(2 * rows, q)
            wide = wfull[i].reshape(q, c.ff)
            part[i, pl.ds(pl.multiple_of(h * 2 * rows, 16), 2 * rows), :] = nn(some, wide).astype(BF16)
            return carry

        lax.fori_loop(0, nx // 2, step, 0)
        part_perm[i, at_y(2)] = permuted(i, at_y(2)).astype(BF16)
        for way in range(2):
            rs_copy(i, way, 0).start()

    def preact_relay(i):
        for way, sign in ((0, 1), (1, -1)):
            j = at_y(sign + NY)
            mine = permuted(i, j)
            ref = rs_a.at[i, way]
            remote(ref, ref, sem_rs, (i, way, 0), to_y(NY - sign)).wait_recv()
            span = slice(way * hb, (way + 1) * hb)
            other = slice((1 - way) * hb, (2 - way) * hb)
            part_perm[i, j, span] = (mine[span] + rs_a[i, way].astype(F32)).astype(BF16)
            part_perm[i, j, other] = mine[other].astype(BF16)
            rs_copy(i, way, 1).start()
        part_perm[i, y] = permuted(i, y).astype(BF16)

    def pg_copy(i, way, s):
        sign = 1 if way == 0 else -1
        if s == 0:
            ref = pre_grad.at[i, y]
        else:
            ref = pre_grad.at[i, at_y(NY - sign), pl.ds(way * hb, hb)]
        return remote(ref, ref, sem_pg, (i, way, s), to_y(sign + NY))

    def pg_recv(i, way, s):
        sign = 1 if way == 0 else -1
        if s == 0:
            ref = pre_grad.at[i, at_y(NY - sign)]
        else:
            ref = pre_grad.at[i, at_y(2), pl.ds(way * hb, hb)]
        remote(ref, ref, sem_pg, (i, way, s), to_y(NY - sign)).wait_recv()

    def make_pre_grad(i):
        for way, sign in ((0, 1), (1, -1)):
            ref = rs_b.at[i, way]
            remote(ref, ref, sem_rs, (i, way, 1), to_y(NY - sign)).wait_recv()
        preact = part_perm[i, y].astype(F32) + rs_b[i, 0].astype(F32) + rs_b[i, 1].astype(F32)
        pre_grad[i, y] = (grad_hidden[i].astype(F32) * silu_slope(preact)).astype(BF16)
        for way in range(2):
            pg_copy(i, way, 0).start()

    def relay_pre_grad(i):
        for way in range(2):
            pg_recv(i, way, 0)
            pg_copy(i, way, 1).start()

    def back_copy(i, d):
        return remote(backs.at[i, at_x(d)], returned.at[i, me], sem_back, (i, d - 1), to_x(d))

    def wg_copy(i, way, s):
        sign = 1 if way == 0 else -1
        src, dst = wg_out.at[i, way, s - 1], wg_in.at[i, way, s - 1]
        if s == 1:
            src, dst = src.at[pl.ds(way * hc, hc)], dst.at[pl.ds(way * hc, hc)]
        return remote(src, dst, sem_wg, (i, way, s - 1), to_z(sign))

    def wg_recv(i, way, s):
        sign = 1 if way == 0 else -1
        ref = wg_in.at[i, way, s - 1]
        if s == 1:
            ref = ref.at[pl.ds(way * hc, hc)]
        remote(ref, ref, sem_wg, (i, way, s - 1), to_z(-sign)).wait_recv()

    def weight_grad(i, owner):
        left = slots[i, :, :, pl.ds(pl.multiple_of(owner * cb, cb), cb)].reshape(m, cb)
        return tn(left, pg_rows[i])

    def wg_step(i, s):
        if s == 1:
            block = weight_grad(i, at_z(half)).astype(BF16)
            for way in range(2):
                span = slice(way * hc, (way + 1) * hc)
                wg_out[i, way, 0, span] = block[span]
                wg_copy(i, way, 1).start()
            return
        for way, sign in ((0, 1), (1, -1)):
            block = weight_grad(i, at_z(sign * (half + 1 - s)))
            wg_recv(i, way, s - 1)
            if s == 2:
                span = slice(way * hc, (way + 1) * hc)
                other = slice((1 - way) * hc, (2 - way) * hc)
                wg_out[i, way, 1, span] = (block[span] + wg_in[i, way, 0, span].astype(F32)).astype(BF16)
                wg_out[i, way, 1, other] = block[other].astype(BF16)
            else:
                wg_out[i, way, s - 1] = (block + wg_in[i, way, s - 2].astype(F32)).astype(BF16)
            wg_copy(i, way, s).start()

    def back_part(i):
        for way in range(2):
            pg_recv(i, way, 1)
        grads = pre_grad[i].reshape(m, c.ff)

        def unpermute(h, carry):
            span = pl.ds(pl.multiple_of(h * 2 * rows, 16), 2 * rows)
            pg_rows[i, span, :] = nn(order_t[span, :], grads).astype(BF16)
            return carry

        lax.fori_loop(0, nx // 2, unpermute, 0)
        wg_step(i, 1)

        def back_rows(owner):
            span = pl.ds(pl.multiple_of(owner * rows, 16), rows)
            out = nt(pg_rows[i, span, :], wfull[i].reshape(q, c.ff)).astype(BF16)
            terms = out.astype(F32) * slots[i, owner].astype(F32)
            gain_acc[...] += jnp.sum(terms.reshape(rows // 8, 8, q), axis=0)
            return out

        def step(d, carry):
            backs[i, at_x(d)] = back_rows(at_x(d))
            back_copy(i, d).start()
            return carry

        lax.fori_loop(1, nx, step, 0)
        returned[i, me] = back_rows(me)

    def combine(i):
        def wait_backs(d, carry):
            ref = returned.at[i, at_x(nx - d)]
            remote(ref, ref, sem_back, (i, d - 1), to_x(nx - d)).wait_recv()
            return carry

        lax.fori_loop(1, nx, wait_backs, 0)
        got = returned[i].reshape(m, q)
        for j in range(NY):
            there = place[i, :, :, j * t : (j + 1) * t].reshape(m, t)
            if i == 0:
                acc[j] = tn(there, got)
            else:
                tok_back[j] = (acc[j] + tn(there, got)).astype(BF16)

    preact_part(0)
    preact_part(1)
    preact_relay(0)
    preact_relay(1)
    make_pre_grad(0)
    make_pre_grad(1)
    relay_pre_grad(0)
    relay_pre_grad(1)
    back_part(0)
    back_part(1)

    ar0[c.e : c.e + 8, :] = gain_acc[...]

    def ar0_slice(e):
        return ar0.at[:, pl.ds(pl.multiple_of(e * cb, cb), cb)]

    def ar_x(d):
        return remote(ar0_slice(at_x(d)), ar1.at[me], sem_ar, (0, d - 1), to_x(d))

    for d in range(1, nx):
        ar_x(d).start()
    ar1[me] = ar0[:, pl.ds(pl.multiple_of(me * cb, cb), cb)]
    wg_step(0, 2)
    wg_step(1, 2)

    def wait_ar(index, ref, target):
        remote(ref, ref, sem_ar, index, target).wait_recv()

    for d in range(1, nx):
        wait_ar((0, d - 1), ar1.at[at_x(nx - d)], to_x(nx - d))
    ar2[z] = jnp.sum(ar1[...], axis=0)

    def ar_z(d):
        return remote(ar2.at[z], ar2.at[z], sem_ar, (1, d - 1), to_z(d))

    for d in range(1, nz):
        ar_z(d).start()
    wg_step(0, 3)
    wg_step(1, 3)
    for d in range(1, nz):
        wait_ar((1, d - 1), ar2.at[at_z(-d)], to_z(-d))
    ar3[y] = jnp.sum(ar2[...], axis=0)

    def ar_y(d):
        return remote(ar3.at[y], ar3.at[y], sem_ar, (2, d - 1), to_y(d))

    for d in range(1, NY):
        ar_y(d).start()
    combine(0)
    for s in range(4, half + 1):
        wg_step(0, s)
        wg_step(1, s)
    for d in range(1, NY):
        wait_ar((2, d - 1), ar3.at[at_y(NY - d)], to_y(NY - d))
    ar4[me] = ar3[...]

    def ar_out(d):
        return remote(ar3, ar4.at[me], sem_ar, (3, d - 1), to_x(d))

    for d in range(1, nx):
        ar_out(d).start()
    combine(1)

    def ret_copy(d):
        return remote(tok_back.at[at_y(d)], tok_ret.at[y], sem_ret, (d - 1,), to_y(d))

    for d in (2, 1, 3):
        ret_copy(d).start()
    tok_ret[y] = tok_back[y]

    for i in range(2):
        block = weight_grad(i, z)
        for way in range(2):
            wg_recv(i, way, half)
        up_out[i] = block + wg_in[i, 0, half - 1].astype(F32) + wg_in[i, 1, half - 1].astype(F32)

    for d in range(1, nx):
        wait_ar((3, d - 1), ar4.at[at_x(nx - d)], to_x(nx - d))
    for e in range(nx):
        for j in range(NY):
            span = slice((e * NY + j) * cb, (e * NY + j + 1) * cb)
            router_out[:, span] = ar4[e, j, 0 : c.e]
            total = jnp.sum(ar4[e, j, c.e : c.e + 8], axis=0, keepdims=True)
            gain_out[:, span] = total / norm_gain[:, span]

    for d in range(1, NY):
        ref = tok_ret.at[at_y(NY - d)]
        remote(ref, ref, sem_ret, (d - 1,), to_y(NY - d)).wait_recv()
    inv = inv_ref[...]
    grads = info[y, 0 : c.e, :].astype(BF16)
    inner = jnp.zeros((t, cb), F32)
    for p in range(NY):
        acc[p] = tn(grads, rw_slices[p]) + tok_ret[p].astype(F32)
    for b in range(nz * NY):
        span = slice(b * cb, (b + 1) * cb)
        here = slice((b // NY) * cb, (b // NY + 1) * cb)
        inner = inner + acc[b % NY, :, here] * norm_gain[:, span] * residual[:, span].astype(F32)
    mean = jnp.sum(inner, axis=1, keepdims=True) * (1.0 / c.d)
    scale = inv * inv * inv * mean
    for b in range(nz * NY):
        span = slice(b * cb, (b + 1) * cb)
        here = slice((b // NY) * cb, (b // NY + 1) * cb)
        scaled = acc[b % NY, :, here] * norm_gain[:, span]
        wide = residual[:, span].astype(F32)
        resid_out[:, span] = (inv * scaled - wide * scale).astype(BF16)

    for i in range(2):
        for way in range(2):
            for s in range(1, half + 1):
                w_copy(i, way, s).wait_send()
                wg_copy(i, way, s).wait_send()
            for s in range(2):
                rs_copy(i, way, s).wait_send()
                pg_copy(i, way, s).wait_send()
        for d in range(1, nx):
            slot_copy(i, d).wait_send()
            back_copy(i, d).wait_send()
    for d in range(1, NY):
        tok_copy(d).wait_send()
        info_copy(d).wait_send()
        ret_copy(d).wait_send()
        ar_y(d).wait_send()
    for d in range(1, nx):
        ar_x(d).wait_send()
        ar_out(d).wait_send()
    for d in range(1, nz):
        ar_z(d).wait_send()


def group_order(c):
    out = np.arange(c.m)
    group, sender, slot = out // c.blk, out % c.blk // c.cap, out % c.cap
    source = sender * c.rows + group * c.cap + slot
    table = np.zeros((c.m, c.m), np.float32)
    table[out, source] = 1.0
    return table


def local(
    mesh, residual, norm_gain, router_weight, up_weight, routes, keep_flags, gate_grad, grad_hidden
):
    c = Dims(
        mesh,
        residual.shape[0],
        residual.shape[1],
        up_weight.shape[2],
        grad_hidden.shape[1] // mesh.shape["expert"],
    )
    order = group_order(c)
    half = c.nz // 2
    dma = pltpu.SemaphoreType.DMA
    most = max(c.nz, c.nx) - 1
    vmem = pl.BlockSpec(memory_space=pltpu.VMEM)
    resid_grad, up_grad, router_grad, gain_grad = pl.pallas_call(
        functools.partial(kernel, c),
        out_shape=(
            jax.ShapeDtypeStruct((c.t, c.d), BF16),
            jax.ShapeDtypeStruct((2, c.cb, c.ff), F32),
            jax.ShapeDtypeStruct((c.e, c.d), F32),
            jax.ShapeDtypeStruct((1, c.d), F32),
        ),
        in_specs=[vmem] * 10,
        out_specs=(vmem,) * 4,
        scratch_shapes=[
            pltpu.VMEM((c.t, c.cb), F32),
            pltpu.VMEM((NY, c.t, c.q), BF16),
            pltpu.VMEM((NY, c.t, c.q), BF16),
            pltpu.VMEM((NY, c.e + 8, c.t), F32),
            pltpu.VMEM((NY, c.e, c.q), BF16),
            pltpu.VMEM((2, c.nx, c.rows, NY * c.t), BF16),
            pltpu.VMEM((2, c.nx, c.rows, c.q), BF16),
            pltpu.VMEM((2, c.nx, c.rows, c.q), BF16),
            pltpu.VMEM((2, c.nz, c.cb, c.ff), BF16),
            pltpu.VMEM((2, c.m, c.ff), BF16),
            pltpu.VMEM((2, NY, c.blk, c.ff), BF16),
            pltpu.VMEM((2, 2, c.blk // 2, c.ff), BF16),
            pltpu.VMEM((2, 2, c.blk, c.ff), BF16),
            pltpu.VMEM((2, NY, c.blk, c.ff), BF16),
            pltpu.VMEM((2, c.m, c.ff), BF16),
            pltpu.VMEM((2, c.nx, c.rows, c.q), BF16),
            pltpu.VMEM((2, c.nx, c.rows, c.q), BF16),
            pltpu.VMEM((2, 2, half, c.cb, c.ff), BF16),
            pltpu.VMEM((2, 2, half, c.cb, c.ff), BF16),
            pltpu.VMEM((NY, c.t, c.q), F32),
            pltpu.VMEM((NY, c.t, c.q), BF16),
            pltpu.VMEM((NY, c.t, c.q), BF16),
            pltpu.VMEM((8, c.q), F32),
            pltpu.VMEM((c.e + 8, c.q), F32),
            pltpu.VMEM((c.nx, c.e + 8, c.cb), F32),
            pltpu.VMEM((c.nz, c.e + 8, c.cb), F32),
            pltpu.VMEM((NY, c.e + 8, c.cb), F32),
            pltpu.VMEM((c.nx, NY, c.e + 8, c.cb), F32),
            dma((2, NY - 1)),
            dma((2, NY - 1)),
            dma((2, 2, c.nx - 1)),
            dma((2, 2, 2, half)),
            dma((2, 2, 2, 2)),
            dma((2, 2, 2, 2)),
            dma((2, 2, c.nx - 1)),
            dma((2, 2, 2, half)),
            dma((2, NY - 1)),
            dma((2, 4, most)),
        ],
        compiler_params=pltpu.CompilerParams(
            collective_id=0, has_side_effects=True, vmem_limit_bytes=60 * 2**20
        ),
        cost_estimate=pl.CostEstimate(
            flops=12 * c.m * c.q * c.ff, bytes_accessed=8 * 2**20, transcendentals=2 * c.blk * c.ff
        ),
    )(
        residual,
        norm_gain.reshape(1, c.d),
        router_weight,
        up_weight.transpose(1, 0, 2),
        routes.T,
        keep_flags.T,
        gate_grad.T,
        grad_hidden,
        jnp.asarray(order, BF16),
        jnp.asarray(order.T, BF16),
    )
    return (resid_grad, up_grad.transpose(1, 0, 2), router_grad, gain_grad.reshape(c.d))


def solution(mesh):
    in_specs = (
        P(("dp", "expert"), None),
        P(),
        P(),
        P("dp", "expert", None),
        P(("dp", "expert"), None),
        P(("dp", "expert"), None),
        P(("dp", "expert"), None),
        P("expert", "dp", None),
    )
    out_specs = (P(("dp", "expert"), None), P("dp", "expert", None), P(), P())
    return jax.shard_map(
        functools.partial(local, mesh), mesh=mesh, in_specs=in_specs, out_specs=out_specs, check_vma=False
    )
```

time: 460 us -> 162 us (0.35)
  waiting for transfers between devices: 242 us -> 0 us
  Pallas kernels: 0 us -> 154 us
  blocking collectives: 112 us -> 0 us
  local copies, waits for them, and re-layouts: 46.3 us -> 6.91 us
  matrix products: 32.4 us -> 0 us
  between operations: 15.7 us -> 0.65 us
  starting transfers between devices: 5.52 us -> 0 us
    pallas_call x0 -> x1, Pallas kernels: none -> 154 us  [local(): pl.pallas_call(functools.partial(kernel, c), out_shape=(jax.ShapeDtypeStr...]
    unnamed x4 -> x0, waiting for transfers between devices: 90.2 us -> none
    psum x1 -> x0, blocking collectives: 74.4 us -> none  [local(): lax.psum((router_part, gain_part), ('dp', 'expert'))]
    all_gather x1 -> x0, waiting for transfers between devices: 73.8 us -> none  [local(): full_weight = lax.all_gather(up_weight, 'dp', axis=0, tiled=True)]
    psum x1 -> x0, waiting for transfers between devices: 47.2 us -> none  [local(): lax.psum((router_part, gain_part), ('dp', 'expert'))]
    all_to_all x1 -> x0, blocking collectives: 37.9 us -> none  [local(): lax.all_to_all(sending, 'expert', split_axis=1, concat_axis=1, tiled=True)]
    dot_general x8 -> x0, matrix products: 32.4 us -> none  [the longest x1 9.15 us: expert_backward(): jnp.einsum('esd,def->esf', slots_in, full_weight, preferred_element_type=...]
    all_to_all x1 -> x0, waiting for transfers between devices: 30.4 us -> none  [local(): lax.all_to_all(leaving, 'expert', split_axis=1, concat_axis=1, tiled=True)]
  transfers between devices with their start and end apart: 4 -> 0, of which waited for: 4 -> 0; matrix products, arithmetic and copies ran while one was open for 10% -> 0% of each run, Pallas kernels for 0% -> 0%
where the time goes in v1:
time: 162 us
  Pallas kernels  154 us (95%)
  local copies, waits for them, and re-layouts  6.91 us (4%)
    pallas_call x1, Pallas kernels, local(): pl.pallas_call(functools.partial(kernel, c), out_shape=(jax.ShapeDtypeStr...  154 us
    unnamed x11, local copies, waits for them, and re-layouts  6.91 us

profile of v1, /device:TPU:1, one launch (start us, length us, event | category | flops | bytes accessed | tf_op | source)
XLA Modules:
  0.0 161.9 jit_solution(7391414388927409344)
XLA Ops:
  0.6 1.8 %copy.17 = bf16[128,2,768]{2,0,1:T(8,128)(2,1)} copy(bf16[128,2,768]{2,1,0:T(2,128)(2,1)} %param.13) | data formatting | bytes 786432 | tf_op args[3]
  2.4 154.4 %shard_map.129 = (bf16[128,4096]{1,0:T(8,128)(2,1)}, f32[2,128,768]{2,1,0:T(8,128)}, f32[16,4096]{1,0:T(8,128)}, f32[1,4096]{1,0:T(1,128)}) custom-call(bf16[128,4096]{1,0:T(8,128)(2,1)} %residual.1, f32[1,4096]{1,0:T(1,128)} %bitcast.12, bf16[16,4096]{1,0:T(8,128)(2,1)} %router_weight.1, bf16[2,128,768]{2,1,0:T(8,128)(2,1)} %bitcast.10, s32[2,128]{1,0:T(2,128)} %bitcast.13, ...), custom_call_target="tpu_custom_call" | custom-call | flops 6039797760 | bytes 8388608 | tf_op jit(solution)/shard_map/pallas_call | solution.py:590
  156.8 0.0 copy-start
  156.8 2.7 %copy.15 = f32[128,2,768]{2,1,0:T(2,128)} copy(f32[128,2,768]{2,0,1:T(8,128)} %bitcast.9) | data formatting | bytes 1572864
  159.5 0.0 copy-done
  159.5 0.0 copy-start.1
  159.5 1.0 copy.21
  160.5 0.1 copy-done.1
  160.6 0.0 copy-start.2
  160.6 0.7 copy.22
  161.3 0.0 copy-done.2
  161.3 0.6 copy.23
Async XLA Ops:
  156.8 2.7 %copy-start = (bf16[128,4096]{1,0:T(8,128)(2,1)S(1)}, bf16[128,4096]{1,0:T(8,128)(2,1)}, u32[]{:S(2)}) copy-start(bf16[128,4096]{1,0:T(8,128)(2,1)} %get-tuple-element.20) | copy-start | bytes 3145732
  159.5 1.1 copy-start.1
  160.6 0.7 copy-start.2

commit v2 on v1

--- a/solution.py
+++ b/solution.py
@@ -55,9 +55,9 @@
     routes,
     keep,
     gate,
-    grad_hidden,
-    order,
-    order_t,
+    grad_hidden_hbm,
+    order_hbm,
+    order_t_hbm,
     resid_out,
     up_out,
     router_out,
@@ -100,9 +100,15 @@
     sem_wg,
     sem_ret,
     sem_ar,
+    order,
+    order_t,
+    grad_hidden,
+    sem_local,
 ):
     nz, nx, t, q, cb, cap, rows, m, blk = c.nz, c.nx, c.t, c.q, c.cb, c.cap, c.rows, c.m, c.blk
     half = nz // 2
+    hq = q // 2
+    hz = nz // 2
     hb = blk // 2
     hc = cb // 2
     dp = lax.axis_index("dp")
@@ -137,6 +143,14 @@
             device_id_type=pl.DeviceIdType.MESH,
         )
 
+    late = [
+        pltpu.make_async_copy(order_hbm, order, sem_local.at[0]),
+        pltpu.make_async_copy(order_t_hbm, order_t, sem_local.at[1]),
+        pltpu.make_async_copy(grad_hidden_hbm, grad_hidden, sem_local.at[2]),
+    ]
+    for copy in late:
+        copy.start()
+
     barrier = pltpu.get_barrier_semaphore()
     for d in range(1, NY):
         pl.semaphore_signal(barrier, inc=1, device_id=to_y(d))
@@ -180,22 +194,30 @@
         sums = sums + x * x
     inv_rms = lax.rsqrt(jnp.sum(sums, axis=1, keepdims=True) * (1.0 / c.d) + 1e-06)
     inv_ref[...] = jnp.broadcast_to(inv_rms, inv_ref.shape)
+
+    def norm_slice(h, p):
+        for b in range(hz):
+            span = pl.ds(pl.multiple_of(((h * hz + b) * NY + p) * cb, cb), cb)
+            x = residual[:, span].astype(F32)
+            tok_send[h, p, :, b * cb : (b + 1) * cb] = (x * inv_rms * norm_gain[:, span]).astype(BF16)
+
+    def tok_copy(h, d):
+        return remote(tok_send.at[h, at_y(d)], tok.at[h, y], sem_tok, (h, d - 1), to_y(d))
+
+    for d in (2, 1, 3):
+        norm_slice(0, at_y(d))
+        tok_copy(0, d).start()
+    norm_slice(0, y)
+    for p in range(NY):
+        norm_slice(1, p)
     for b in range(nz * NY):
-        span = slice(b * cb, (b + 1) * cb)
         inner = slice((b // NY) * cb, (b // NY + 1) * cb)
-        x = residual[:, span].astype(F32)
-        tok_send[b % NY, :, inner] = (x * inv_rms * norm_gain[:, span]).astype(BF16)
-        rw_slices[b % NY, :, inner] = router_weight[:, span]
-
-    def tok_copy(d):
-        return remote(tok_send.at[at_y(d)], tok.at[y], sem_tok, (d - 1,), to_y(d))
-
-    for d in (2, 1, 3):
-        tok_copy(d).start()
+        rw_slices[b % NY, :, inner] = router_weight[:, b * cb : (b + 1) * cb]
 
     logits = jnp.zeros((c.e, t), F32)
     for p in range(NY):
-        logits = logits + nt(rw_slices[p], tok_send[p])
+        for h in range(2):
+            logits = logits + nt(rw_slices[p, :, h * hq : (h + 1) * hq], tok_send[h, p])
     top = jnp.max(logits, axis=0, keepdims=True)
     expo = jnp.exp(logits - top)
     probs = expo / jnp.sum(expo, axis=0, keepdims=True)
@@ -222,54 +244,66 @@
 
     for d in (2, 1, 3):
         info_copy(d).start()
-    tok[y] = tok_send[y]
+    for d in (2, 1, 3):
+        tok_copy(1, d).start()
+    for h in range(2):
+        tok[h, y] = tok_send[h, y]
     w_step(2)
     for d in range(1, NY):
         ref = info.at[at_y(-d)]
         remote(ref, ref, sem_info, (d - 1,), to_y(-d)).wait_recv()
-    for d in range(1, NY):
-        ref = tok.at[at_y(-d)]
-        remote(ref, ref, sem_tok, (d - 1,), to_y(-d)).wait_recv()
-
-    def slot_copy(i, d):
-        return remote(slots_out.at[i, at_x(d)], slots.at[i, me], sem_slot, (i, d - 1), to_x(d))
-
-    def make_slots(i):
+
+    def wait_tok(h):
+        for d in range(1, NY):
+            ref = tok.at[h, at_y(-d)]
+            remote(ref, ref, sem_tok, (h, d - 1), to_y(-d)).wait_recv()
+
+    def slot_copy(i, h, d):
+        return remote(slots_out.at[i, h, at_x(d)], slots.at[i, h, me], sem_slot, (i, h, d - 1), to_x(d))
+
+    def make_slots(i, h):
         targets = [
             jnp.concatenate([info[j, c.e + k : c.e + k + 1, :] for j in range(NY)], axis=1)
             for k in range(2)
         ]
-        tokens = tok[...].reshape(NY * t, q)
-
-        def place_rows(owner):
-            row = lax.broadcasted_iota(jnp.int32, (rows, NY * t), 0) + (i * m + owner * rows)
-            row = row.astype(F32)
-            hit = (row == targets[0]) | (row == targets[1])
-            placed = jnp.where(hit, 1.0, 0.0).astype(BF16)
-            place[i, owner] = placed
-            return nn(placed, tokens).astype(BF16)
+        tokens = tok[h].reshape(NY * t, hq)
+
+        def slot_rows(owner):
+            if h == 0:
+                row = lax.broadcasted_iota(jnp.int32, (rows, NY * t), 0) + (i * m + owner * rows)
+                row = row.astype(F32)
+                hit = (row == targets[0]) | (row == targets[1])
+                place[i, owner] = jnp.where(hit, 1.0, 0.0).astype(BF16)
+            return nn(place[i, owner], tokens).astype(BF16)
 
         def step(d, carry):
-            slots_out[i, at_x(d)] = place_rows(at_x(d))
-            slot_copy(i, d).start()
+            slots_out[i, h, at_x(d)] = slot_rows(at_x(d))
+            slot_copy(i, h, d).start()
             return carry
 
         lax.fori_loop(1, nx, step, 0)
-        slots[i, me] = place_rows(me)
-
-    make_slots(0)
-    w_step(3)
-    make_slots(1)
-    for s in range(4, half + 1):
+        slots[i, h, me] = slot_rows(me)
+
+    wait_tok(0)
+    make_slots(0, 0)
+    wait_tok(1)
+    make_slots(0, 1)
+    make_slots(1, 0)
+    make_slots(1, 1)
+    for s in range(3, half + 1):
         w_step(s)
 
     lg_all = jnp.concatenate([info[j, 0 : c.e, :] for j in range(NY)], axis=1).astype(BF16)
-    tokens = tok[...].reshape(NY * t, q)
-    ar0[0 : c.e, :] = nn(lg_all, tokens)
-    gain_acc[...] = jnp.zeros_like(gain_acc)
-    for j in range(NY):
-        back = tn(info[j, 0 : c.e, :].astype(BF16), rw_slices[y]) * tok[j].astype(F32)
-        gain_acc[...] += jnp.sum(back.reshape(t // 8, 8, q), axis=0)
+    for h in range(2):
+        span = slice(h * hq, (h + 1) * hq)
+        ar0[0 : c.e, span] = nn(lg_all, tok[h].reshape(NY * t, hq))
+        total = jnp.zeros((8, hq), F32)
+        for j in range(NY):
+            back = tn(info[j, 0 : c.e, :].astype(BF16), rw_slices[y, :, span]) * tok[h, j].astype(F32)
+            total = total + jnp.sum(back.reshape(t // 8, 8, hq), axis=0)
+        gain_acc[:, span] = total
+    for copy in late:
+        copy.wait()
 
     def rs_copy(i, way, s):
         sign = 1 if way == 0 else -1
@@ -290,16 +324,19 @@
                 w_recv(i, way, s)
 
         def wait_slots(d, carry):
-            ref = slots.at[i, at_x(nx - d)]
-            remote(ref, ref, sem_slot, (i, d - 1), to_x(nx - d)).wait_recv()
+            for h in range(2):
+                ref = slots.at[i, h, at_x(nx - d)]
+                remote(ref, ref, sem_slot, (i, h, d - 1), to_x(nx - d)).wait_recv()
             return carry
 
         lax.fori_loop(1, nx, wait_slots, 0)
 
         def step(h, carry):
-            some = slots[i, pl.ds(2 * h, 2)].reshape(2 * rows, q)
-            wide = wfull[i].reshape(q, c.ff)
-            part[i, pl.ds(pl.multiple_of(h * 2 * rows, 16), 2 * rows), :] = nn(some, wide).astype(BF16)
+            total = jnp.zeros((2 * rows, c.ff), F32)
+            for side in range(2):
+                some = slots[i, side, pl.ds(2 * h, 2)].reshape(2 * rows, hq)
+                total = total + nn(some, wfull[i, side * hz : (side + 1) * hz].reshape(hq, c.ff))
+            part[i, pl.ds(pl.multiple_of(h * 2 * rows, 16), 2 * rows), :] = total.astype(BF16)
             return carry
 
         lax.fori_loop(0, nx // 2, step, 0)
@@ -350,8 +387,8 @@
             pg_recv(i, way, 0)
             pg_copy(i, way, 1).start()
 
-    def back_copy(i, d):
-        return remote(backs.at[i, at_x(d)], returned.at[i, me], sem_back, (i, d - 1), to_x(d))
+    def back_copy(i, h, d):
+        return remote(backs.at[i, h, at_x(d)], returned.at[i, h, me], sem_back, (i, h, d - 1), to_x(d))
 
     def wg_copy(i, way, s):
         sign = 1 if way == 0 else -1
@@ -368,7 +405,8 @@
         remote(ref, ref, sem_wg, (i, way, s - 1), to_z(-sign)).wait_recv()
 
     def weight_grad(i, owner):
-        left = slots[i, :, :, pl.ds(pl.multiple_of(owner * cb, cb), cb)].reshape(m, cb)
+        inside = pl.ds(pl.multiple_of((owner % hz) * cb, cb), cb)
+        left = slots[i, owner // hz, :, :, inside].reshape(m, cb)
         return tn(left, pg_rows[i])
 
     def wg_step(i, s):
@@ -402,47 +440,62 @@
             return carry
 
         lax.fori_loop(0, nx // 2, unpermute, 0)
-        wg_step(i, 1)
-
-        def back_rows(owner):
-            span = pl.ds(pl.multiple_of(owner * rows, 16), rows)
-            out = nt(pg_rows[i, span, :], wfull[i].reshape(q, c.ff)).astype(BF16)
-            terms = out.astype(F32) * slots[i, owner].astype(F32)
-            gain_acc[...] += jnp.sum(terms.reshape(rows // 8, 8, q), axis=0)
-            return out
-
+        wide = 2 * cb
+        for h in range(2):
+            for b in range(hq // wide):
+                span = slice(b * wide, (b + 1) * wide)
+                first = h * hz + 2 * b
+                out = nt(pg_rows[i], wfull[i, first : first + 2].reshape(wide, c.ff)).astype(BF16)
+                backs[i, h, :, :, span] = out.reshape(nx, rows, wide)
+                terms = out.astype(F32) * slots[i, h, :, :, span].reshape(m, wide).astype(F32)
+                where = slice(h * hq + b * wide, h * hq + (b + 1) * wide)
+                gain_acc[:, where] += jnp.sum(terms.reshape(m // 8, 8, wide), axis=0)
+            if i == 0:
+                send_backs(i, h)
+            if h == 0:
+                wg_step(i, 1)
+
+    def send_backs(i, h):
         def step(d, carry):
-            backs[i, at_x(d)] = back_rows(at_x(d))
-            back_copy(i, d).start()
+            back_copy(i, h, d).start()
             return carry
 
         lax.fori_loop(1, nx, step, 0)
-        returned[i, me] = back_rows(me)
-
-    def combine(i):
+        returned[i, h, me] = backs[i, h, me]
+
+    def combine(i, h):
         def wait_backs(d, carry):
-            ref = returned.at[i, at_x(nx - d)]
-            remote(ref, ref, sem_back, (i, d - 1), to_x(nx - d)).wait_recv()
+            ref = returned.at[i, h, at_x(nx - d)]
+            remote(ref, ref, sem_back, (i, h, d - 1), to_x(nx - d)).wait_recv()
             return carry
 
         lax.fori_loop(1, nx, wait_backs, 0)
-        got = returned[i].reshape(m, q)
+        got = returned[i, h].reshape(m, hq)
+        span = slice(h * hq, (h + 1) * hq)
         for j in range(NY):
             there = place[i, :, :, j * t : (j + 1) * t].reshape(m, t)
             if i == 0:
-                acc[j] = tn(there, got)
+                acc[j, :, span] = tn(there, got)
             else:
-                tok_back[j] = (acc[j] + tn(there, got)).astype(BF16)
+                tok_back[h, j] = (acc[j, :, span] + tn(there, got)).astype(BF16)
+
+    def ret_copy(h, d):
+        return remote(tok_back.at[h, at_y(d)], tok_ret.at[h, y], sem_ret, (h, d - 1), to_y(d))
+
+    def send_ret(h):
+        for d in (2, 1, 3):
+            ret_copy(h, d).start()
+        tok_ret[h, y] = tok_back[h, y]
 
     preact_part(0)
+    preact_relay(0)
     preact_part(1)
-    preact_relay(0)
+    make_pre_grad(0)
     preact_relay(1)
-    make_pre_grad(0)
+    relay_pre_grad(0)
     make_pre_grad(1)
-    relay_pre_grad(0)
+    back_part(0)
     relay_pre_grad(1)
-    back_part(0)
     back_part(1)
 
     ar0[c.e : c.e + 8, :] = gain_acc[...]
@@ -455,6 +508,8 @@
 
     for d in range(1, nx):
         ar_x(d).start()
+    send_backs(1, 0)
+    send_backs(1, 1)
     ar1[me] = ar0[:, pl.ds(pl.multiple_of(me * cb, cb), cb)]
     wg_step(0, 2)
     wg_step(1, 2)
@@ -482,7 +537,8 @@
 
     for d in range(1, NY):
         ar_y(d).start()
-    combine(0)
+    for h in range(2):
+        combine(0, h)
     for s in range(4, half + 1):
         wg_step(0, s)
         wg_step(1, s)
@@ -495,20 +551,15 @@
 
     for d in range(1, nx):
         ar_out(d).start()
-    combine(1)
-
-    def ret_copy(d):
-        return remote(tok_back.at[at_y(d)], tok_ret.at[y], sem_ret, (d - 1,), to_y(d))
-
-    for d in (2, 1, 3):
-        ret_copy(d).start()
-    tok_ret[y] = tok_back[y]
+    for h in range(2):
+        combine(1, h)
+        send_ret(h)
 
     for i in range(2):
         block = weight_grad(i, z)
         for way in range(2):
             wg_recv(i, way, half)
-        up_out[i] = block + wg_in[i, 0, half - 1].astype(F32) + wg_in[i, 1, half - 1].astype(F32)
+        up_out[:, i, :] = block + wg_in[i, 0, half - 1].astype(F32) + wg_in[i, 1, half - 1].astype(F32)
 
     for d in range(1, nx):
         wait_ar((3, d - 1), ar4.at[at_x(nx - d)], to_x(nx - d))
@@ -519,18 +570,20 @@
             total = jnp.sum(ar4[e, j, c.e : c.e + 8], axis=0, keepdims=True)
             gain_out[:, span] = total / norm_gain[:, span]
 
-    for d in range(1, NY):
-        ref = tok_ret.at[at_y(NY - d)]
-        remote(ref, ref, sem_ret, (d - 1,), to_y(NY - d)).wait_recv()
     inv = inv_ref[...]
     grads = info[y, 0 : c.e, :].astype(BF16)
     inner = jnp.zeros((t, cb), F32)
-    for p in range(NY):
-        acc[p] = tn(grads, rw_slices[p]) + tok_ret[p].astype(F32)
-    for b in range(nz * NY):
-        span = slice(b * cb, (b + 1) * cb)
-        here = slice((b // NY) * cb, (b // NY + 1) * cb)
-        inner = inner + acc[b % NY, :, here] * norm_gain[:, span] * residual[:, span].astype(F32)
+    for h in range(2):
+        for d in range(1, NY):
+            ref = tok_ret.at[h, at_y(NY - d)]
+            remote(ref, ref, sem_ret, (h, d - 1), to_y(NY - d)).wait_recv()
+        for p in range(NY):
+            half_span = slice(h * hq, (h + 1) * hq)
+            acc[p, :, half_span] = tn(grads, rw_slices[p, :, half_span]) + tok_ret[h, p].astype(F32)
+        for b in range(h * hz * NY, (h + 1) * hz * NY):
+            span = slice(b * cb, (b + 1) * cb)
+            here = slice((b // NY) * cb, (b // NY + 1) * cb)
+            inner = inner + acc[b % NY, :, here] * norm_gain[:, span] * residual[:, span].astype(F32)
     mean = jnp.sum(inner, axis=1, keepdims=True) * (1.0 / c.d)
     scale = inv * inv * inv * mean
     for b in range(nz * NY):
@@ -548,13 +601,15 @@
             for s in range(2):
                 rs_copy(i, way, s).wait_send()
                 pg_copy(i, way, s).wait_send()
-        for d in range(1, nx):
-            slot_copy(i, d).wait_send()
-            back_copy(i, d).wait_send()
+        for h in range(2):
+            for d in range(1, nx):
+                slot_copy(i, h, d).wait_send()
+                back_copy(i, h, d).wait_send()
     for d in range(1, NY):
-        tok_copy(d).wait_send()
+        for h in range(2):
+            tok_copy(h, d).wait_send()
+            ret_copy(h, d).wait_send()
         info_copy(d).wait_send()
-        ret_copy(d).wait_send()
         ar_y(d).wait_send()
     for d in range(1, nx):
         ar_x(d).wait_send()
@@ -591,21 +646,21 @@
         functools.partial(kernel, c),
         out_shape=(
             jax.ShapeDtypeStruct((c.t, c.d), BF16),
-            jax.ShapeDtypeStruct((2, c.cb, c.ff), F32),
+            jax.ShapeDtypeStruct((c.cb, 2, c.ff), F32),
             jax.ShapeDtypeStruct((c.e, c.d), F32),
             jax.ShapeDtypeStruct((1, c.d), F32),
         ),
-        in_specs=[vmem] * 10,
+        in_specs=[vmem] * 7 + [pl.BlockSpec(memory_space=pl.ANY)] * 3,
         out_specs=(vmem,) * 4,
         scratch_shapes=[
             pltpu.VMEM((c.t, c.cb), F32),
-            pltpu.VMEM((NY, c.t, c.q), BF16),
-            pltpu.VMEM((NY, c.t, c.q), BF16),
+            pltpu.VMEM((2, NY, c.t, c.q // 2), BF16),
+            pltpu.VMEM((2, NY, c.t, c.q // 2), BF16),
             pltpu.VMEM((NY, c.e + 8, c.t), F32),
             pltpu.VMEM((NY, c.e, c.q), BF16),
             pltpu.VMEM((2, c.nx, c.rows, NY * c.t), BF16),
-            pltpu.VMEM((2, c.nx, c.rows, c.q), BF16),
-            pltpu.VMEM((2, c.nx, c.rows, c.q), BF16),
+            pltpu.VMEM((2, 2, c.nx, c.rows, c.q // 2), BF16),
+            pltpu.VMEM((2, 2, c.nx, c.rows, c.q // 2), BF16),
             pltpu.VMEM((2, c.nz, c.cb, c.ff), BF16),
             pltpu.VMEM((2, c.m, c.ff), BF16),
             pltpu.VMEM((2, NY, c.blk, c.ff), BF16),
@@ -613,29 +668,33 @@
             pltpu.VMEM((2, 2, c.blk, c.ff), BF16),
             pltpu.VMEM((2, NY, c.blk, c.ff), BF16),
             pltpu.VMEM((2, c.m, c.ff), BF16),
-            pltpu.VMEM((2, c.nx, c.rows, c.q), BF16),
-            pltpu.VMEM((2, c.nx, c.rows, c.q), BF16),
+            pltpu.VMEM((2, 2, c.nx, c.rows, c.q // 2), BF16),
+            pltpu.VMEM((2, 2, c.nx, c.rows, c.q // 2), BF16),
             pltpu.VMEM((2, 2, half, c.cb, c.ff), BF16),
             pltpu.VMEM((2, 2, half, c.cb, c.ff), BF16),
             pltpu.VMEM((NY, c.t, c.q), F32),
-            pltpu.VMEM((NY, c.t, c.q), BF16),
-            pltpu.VMEM((NY, c.t, c.q), BF16),
+            pltpu.VMEM((2, NY, c.t, c.q // 2), BF16),
+            pltpu.VMEM((2, NY, c.t, c.q // 2), BF16),
             pltpu.VMEM((8, c.q), F32),
             pltpu.VMEM((c.e + 8, c.q), F32),
             pltpu.VMEM((c.nx, c.e + 8, c.cb), F32),
             pltpu.VMEM((c.nz, c.e + 8, c.cb), F32),
             pltpu.VMEM((NY, c.e + 8, c.cb), F32),
             pltpu.VMEM((c.nx, NY, c.e + 8, c.cb), F32),
+            dma((2, 2, NY - 1)),
             dma((2, NY - 1)),
-            dma((2, NY - 1)),
-            dma((2, 2, c.nx - 1)),
+            dma((2, 2, 2, c.nx - 1)),
             dma((2, 2, 2, half)),
             dma((2, 2, 2, 2)),
             dma((2, 2, 2, 2)),
-            dma((2, 2, c.nx - 1)),
+            dma((2, 2, 2, c.nx - 1)),
             dma((2, 2, 2, half)),
-            dma((2, NY - 1)),
+            dma((2, 2, NY - 1)),
             dma((2, 4, most)),
+            pltpu.VMEM((c.m, c.m), BF16),
+            pltpu.VMEM((c.m, c.m), BF16),
+            pltpu.VMEM((2, c.blk, c.ff), BF16),
+            dma((3,)),
         ],
         compiler_params=pltpu.CompilerParams(
             collective_id=0, has_side_effects=True, vmem_limit_bytes=60 * 2**20
@@ -655,7 +714,7 @@
         jnp.asarray(order, BF16),
         jnp.asarray(order.T, BF16),
     )
-    return (resid_grad, up_grad.transpose(1, 0, 2), router_grad, gain_grad.reshape(c.d))
+    return (resid_grad, up_grad, router_grad, gain_grad.reshape(c.d))
 
 
 def solution(mesh):

time: 162 us -> 135 us (0.83)
  the two profiles are of different devices: /device:TPU:1 before, /device:TPU:10 now
where the time goes in v2:
time: 135 us; the launch traced here: 134 us
  Pallas kernels  127 us (94%)
  local copies, waits for them, and re-layouts  6.56 us (5%)
    pallas_call x1, Pallas kernels, local(): pl.pallas_call(functools.partial(kernel, c), out_shape=(jax.ShapeDtypeStr...  127 us
    unnamed x11, local copies, waits for them, and re-layouts  6.56 us

profile of v2, /device:TPU:10, one launch (start us, length us, event | category | flops | bytes accessed | tf_op | source)
XLA Modules:
  0.0 134.3 jit_solution(16513259695646671306)
XLA Ops:
  0.6 1.8 %copy.16 = bf16[128,2,768]{2,0,1:T(8,128)(2,1)} copy(bf16[128,2,768]{2,1,0:T(2,128)(2,1)} %param.13) | data formatting | bytes 786432 | tf_op args[3]
  2.4 127.1 %shard_map.129 = (bf16[128,4096]{1,0:T(8,128)(2,1)}, f32[128,2,768]{2,1,0:T(2,128)}, f32[16,4096]{1,0:T(8,128)}, f32[1,4096]{1,0:T(1,128)}) custom-call(bf16[128,4096]{1,0:T(8,128)(2,1)} %residual.1, f32[1,4096]{1,0:T(1,128)} %bitcast.10, bf16[16,4096]{1,0:T(8,128)(2,1)} %router_weight.1, bf16[2,128,768]{2,1,0:T(8,128)(2,1)} %bitcast.8, s32[2,128]{1,0:T(2,128)} %bitcast.11, ...), custom_call_target="tpu_custom_call" | custom-call | flops 6039797760 | bytes 8388608 | tf_op jit(solution)/shard_map/pallas_call | solution.py:645
  129.5 0.0 copy-start
  129.5 2.4 %copy.21 = bf16[128,4096]{1,0:T(8,128)(2,1)} copy(bf16[128,4096]{1,0:T(8,128)(2,1)} %get-tuple-element.16) | data formatting | bytes 2097152
  131.9 0.0 copy-done
  131.9 0.0 copy-start.1
  131.9 0.9 copy.22
  132.8 0.2 copy-done.1
  133.0 0.0 copy-start.2
  133.0 0.7 copy.23
  133.7 0.0 copy-done.2
  133.7 0.6 copy.24
Async XLA Ops:
  129.5 2.4 %copy-start = (f32[128,2,768]{2,1,0:T(2,128)S(1)}, f32[128,2,768]{2,1,0:T(2,128)}, u32[]{:S(2)}) copy-start(f32[128,2,768]{2,1,0:T(2,128)} %get-tuple-element.17) | copy-start | bytes 2359300
  131.9 1.1 copy-start.1
  133.0 0.7 copy-start.2

commit v3 on v2

--- a/solution.py
+++ b/solution.py
@@ -48,10 +48,10 @@
 
 def kernel(
     c,
-    residual,
+    residual_hbm,
     norm_gain,
     router_weight,
-    weight,
+    weight_hbm,
     routes,
     keep,
     gate,
@@ -103,6 +103,8 @@
     order,
     order_t,
     grad_hidden,
+    residual,
+    wg_own,
     sem_local,
 ):
     nz, nx, t, q, cb, cap, rows, m, blk = c.nz, c.nx, c.t, c.q, c.cb, c.cap, c.rows, c.m, c.blk
@@ -143,14 +145,18 @@
             device_id_type=pl.DeviceIdType.MESH,
         )
 
+    early = [
+        pltpu.make_async_copy(weight_hbm.at[0], wfull.at[0, z], sem_local.at[3]),
+        pltpu.make_async_copy(weight_hbm.at[1], wfull.at[1, z], sem_local.at[4]),
+        pltpu.make_async_copy(residual_hbm, residual, sem_local.at[5]),
+    ]
+    for copy in early:
+        copy.start()
     late = [
         pltpu.make_async_copy(order_hbm, order, sem_local.at[0]),
         pltpu.make_async_copy(order_t_hbm, order_t, sem_local.at[1]),
         pltpu.make_async_copy(grad_hidden_hbm, grad_hidden, sem_local.at[2]),
     ]
-    for copy in late:
-        copy.start()
-
     barrier = pltpu.get_barrier_semaphore()
     for d in range(1, NY):
         pl.semaphore_signal(barrier, inc=1, device_id=to_y(d))
@@ -160,33 +166,33 @@
         pl.semaphore_signal(barrier, inc=1, device_id=to_x(d))
     pl.semaphore_wait(barrier, NY + nz + nx - 3)
 
-    for i in range(2):
-        wfull[i, z] = weight[i]
-
-    def w_copy(i, way, s):
+    def w_piece(i, way, s, piece, source):
         sign = 1 if way == 0 else -1
-        source = at_z(-sign * (s - 1))
-        ref = wfull.at[i, source]
-        if s == half:
-            ref = ref.at[pl.ds(way * hc, hc)]
-        return remote(ref, ref, sem_w, (i, way, s - 1), to_z(sign))
-
-    def w_recv(i, way, s):
+        ref = wfull.at[i, source, pl.ds(piece * hc, hc)]
+        return remote(ref, ref, sem_w, (i, way, s - 1, piece), to_z(sign))
+
+    def w_copy(i, way, s, piece):
         sign = 1 if way == 0 else -1
-        ref = wfull.at[i, at_z(-sign * s)]
-        if s == half:
-            ref = ref.at[pl.ds(way * hc, hc)]
-        remote(ref, ref, sem_w, (i, way, s - 1), to_z(-sign)).wait_recv()
-
-    def w_step(s):
-        for i in range(2):
-            for way in range(2):
-                if s > 1:
-                    w_recv(i, way, s - 1)
-                if s <= half:
-                    w_copy(i, way, s).start()
-
-    w_step(1)
+        return w_piece(i, way, s, piece, at_z(-sign * (s - 1)))
+
+    def w_recv(i, way, s, piece):
+        sign = 1 if way == 0 else -1
+        w_piece(i, way, s, piece, at_z(-sign * s)).wait_recv()
+
+    def w_step(i, s, piece):
+        for way in range(2):
+            if s > 1:
+                w_recv(i, way, s - 1, piece)
+            if s < half or way == piece:
+                w_copy(i, way, s, piece).start()
+
+    early[0].wait()
+    w_step(0, 1, 0)
+    w_step(0, 1, 1)
+    early[1].wait()
+    early[2].wait()
+    for copy in late:
+        copy.start()
 
     sums = jnp.zeros((t, cb), F32)
     for b in range(nz * NY):
@@ -208,6 +214,7 @@
         norm_slice(0, at_y(d))
         tok_copy(0, d).start()
     norm_slice(0, y)
+    w_step(0, 2, 0)
     for p in range(NY):
         norm_slice(1, p)
     for b in range(nz * NY):
@@ -248,7 +255,10 @@
         tok_copy(1, d).start()
     for h in range(2):
         tok[h, y] = tok_send[h, y]
-    w_step(2)
+    w_step(0, 2, 1)
+    for s in range(3, half):
+        for piece in range(2):
+            w_step(0, s, piece)
     for d in range(1, NY):
         ref = info.at[at_y(-d)]
         remote(ref, ref, sem_info, (d - 1,), to_y(-d)).wait_recv()
@@ -286,12 +296,19 @@
 
     wait_tok(0)
     make_slots(0, 0)
+    for piece in range(2):
+        w_step(0, half, piece)
+    for piece in range(2):
+        w_step(1, 1, piece)
     wait_tok(1)
     make_slots(0, 1)
+    w_step(1, 2, 0)
     make_slots(1, 0)
+    w_step(1, 2, 1)
     make_slots(1, 1)
-    for s in range(3, half + 1):
-        w_step(s)
+    for s in range(3, half):
+        for piece in range(2):
+            w_step(1, s, piece)
 
     lg_all = jnp.concatenate([info[j, 0 : c.e, :] for j in range(NY)], axis=1).astype(BF16)
     for h in range(2):
@@ -319,9 +336,8 @@
         return nn(order[pl.ds(pl.multiple_of(j * blk, 16), blk), :], part[i])
 
     def preact_part(i):
-        for s in range(half, half + 1):
-            for way in range(2):
-                w_recv(i, way, s)
+        for way in range(2):
+            w_recv(i, way, half, way)
 
         def wait_slots(d, carry):
             for h in range(2):
@@ -487,79 +503,77 @@
             ret_copy(h, d).start()
         tok_ret[h, y] = tok_back[h, y]
 
-    preact_part(0)
-    preact_relay(0)
-    preact_part(1)
-    make_pre_grad(0)
-    preact_relay(1)
-    relay_pre_grad(0)
-    make_pre_grad(1)
-    back_part(0)
-    relay_pre_grad(1)
-    back_part(1)
-
-    ar0[c.e : c.e + 8, :] = gain_acc[...]
-
     def ar0_slice(e):
         return ar0.at[:, pl.ds(pl.multiple_of(e * cb, cb), cb)]
 
     def ar_x(d):
         return remote(ar0_slice(at_x(d)), ar1.at[me], sem_ar, (0, d - 1), to_x(d))
 
+    def ar_z(d):
+        return remote(ar2.at[z], ar2.at[z], sem_ar, (1, d - 1), to_z(d))
+
+    def ar_y(d):
+        return remote(ar3.at[y], ar3.at[y], sem_ar, (2, d - 1), to_y(d))
+
+    def ar_out(d):
+        return remote(ar3, ar4.at[me], sem_ar, (3, d - 1), to_x(d))
+
+    def wait_ar(index, ref, target):
+        remote(ref, ref, sem_ar, index, target).wait_recv()
+
+    preact_part(0)
+    for piece in range(2):
+        w_step(1, half, piece)
+    preact_relay(0)
+    make_pre_grad(0)
+    preact_part(1)
+    relay_pre_grad(0)
+    preact_relay(1)
+    back_part(0)
+    make_pre_grad(1)
+    wg_step(0, 2)
+    relay_pre_grad(1)
+    wg_step(0, 3)
+    back_part(1)
+
+    ar0[c.e : c.e + 8, :] = gain_acc[...]
     for d in range(1, nx):
         ar_x(d).start()
     send_backs(1, 0)
     send_backs(1, 1)
     ar1[me] = ar0[:, pl.ds(pl.multiple_of(me * cb, cb), cb)]
-    wg_step(0, 2)
-    wg_step(1, 2)
-
-    def wait_ar(index, ref, target):
-        remote(ref, ref, sem_ar, index, target).wait_recv()
-
+    for s in range(4, half + 1):
+        wg_step(0, s)
+    for h in range(2):
+        combine(0, h)
     for d in range(1, nx):
         wait_ar((0, d - 1), ar1.at[at_x(nx - d)], to_x(nx - d))
     ar2[z] = jnp.sum(ar1[...], axis=0)
-
-    def ar_z(d):
-        return remote(ar2.at[z], ar2.at[z], sem_ar, (1, d - 1), to_z(d))
-
     for d in range(1, nz):
         ar_z(d).start()
-    wg_step(0, 3)
-    wg_step(1, 3)
+    wg_step(1, 2)
     for d in range(1, nz):
         wait_ar((1, d - 1), ar2.at[at_z(-d)], to_z(-d))
     ar3[y] = jnp.sum(ar2[...], axis=0)
-
-    def ar_y(d):
-        return remote(ar3.at[y], ar3.at[y], sem_ar, (2, d - 1), to_y(d))
-
     for d in range(1, NY):
         ar_y(d).start()
-    for h in range(2):
-        combine(0, h)
-    for s in range(4, half + 1):
-        wg_step(0, s)
-        wg_step(1, s)
+    combine(1, 0)
+    send_ret(0)
+    wg_step(1, 3)
     for d in range(1, NY):
         wait_ar((2, d - 1), ar3.at[at_y(NY - d)], to_y(NY - d))
     ar4[me] = ar3[...]
-
-    def ar_out(d):
-        return remote(ar3, ar4.at[me], sem_ar, (3, d - 1), to_x(d))
-
     for d in range(1, nx):
         ar_out(d).start()
-    for h in range(2):
-        combine(1, h)
-        send_ret(h)
-
     for i in range(2):
-        block = weight_grad(i, z)
-        for way in range(2):
-            wg_recv(i, way, half)
-        up_out[:, i, :] = block + wg_in[i, 0, half - 1].astype(F32) + wg_in[i, 1, half - 1].astype(F32)
+        wg_own[i] = weight_grad(i, z)
+    for s in range(4, half + 1):
+        wg_step(1, s)
+    for way in range(2):
+        wg_recv(0, way, half)
+    up_out[:, 0, :] = wg_own[0] + wg_in[0, 0, half - 1].astype(F32) + wg_in[0, 1, half - 1].astype(F32)
+    combine(1, 1)
+    send_ret(1)
 
     for d in range(1, nx):
         wait_ar((3, d - 1), ar4.at[at_x(nx - d)], to_x(nx - d))
@@ -574,6 +588,10 @@
     grads = info[y, 0 : c.e, :].astype(BF16)
     inner = jnp.zeros((t, cb), F32)
     for h in range(2):
+        if h == 1:
+            for way in range(2):
+                wg_recv(1, way, half)
+            up_out[:, 1, :] = wg_own[1] + wg_in[1, 0, half - 1].astype(F32) + wg_in[1, 1, half - 1].astype(F32)
         for d in range(1, NY):
             ref = tok_ret.at[h, at_y(NY - d)]
             remote(ref, ref, sem_ret, (h, d - 1), to_y(NY - d)).wait_recv()
@@ -596,7 +614,9 @@
     for i in range(2):
         for way in range(2):
             for s in range(1, half + 1):
-                w_copy(i, way, s).wait_send()
+                for piece in range(2):
+                    if s < half or way == piece:
+                        w_copy(i, way, s, piece).wait_send()
                 wg_copy(i, way, s).wait_send()
             for s in range(2):
                 rs_copy(i, way, s).wait_send()
@@ -642,6 +662,7 @@
     dma = pltpu.SemaphoreType.DMA
     most = max(c.nz, c.nx) - 1
     vmem = pl.BlockSpec(memory_space=pltpu.VMEM)
+    hbm = pl.BlockSpec(memory_space=pl.ANY)
     resid_grad, up_grad, router_grad, gain_grad = pl.pallas_call(
         functools.partial(kernel, c),
         out_shape=(
@@ -650,7 +671,7 @@
             jax.ShapeDtypeStruct((c.e, c.d), F32),
             jax.ShapeDtypeStruct((1, c.d), F32),
         ),
-        in_specs=[vmem] * 7 + [pl.BlockSpec(memory_space=pl.ANY)] * 3,
+        in_specs=[hbm, vmem, vmem, hbm, vmem, vmem, vmem, hbm, hbm, hbm],
         out_specs=(vmem,) * 4,
         scratch_shapes=[
             pltpu.VMEM((c.t, c.cb), F32),
@@ -684,7 +705,7 @@
             dma((2, 2, NY - 1)),
             dma((2, NY - 1)),
             dma((2, 2, 2, c.nx - 1)),
-            dma((2, 2, 2, half)),
+            dma((2, 2, 2, half, 2)),
             dma((2, 2, 2, 2)),
             dma((2, 2, 2, 2)),
             dma((2, 2, 2, c.nx - 1)),
@@ -694,7 +715,9 @@
             pltpu.VMEM((c.m, c.m), BF16),
             pltpu.VMEM((c.m, c.m), BF16),
             pltpu.VMEM((2, c.blk, c.ff), BF16),
-            dma((3,)),
+            pltpu.VMEM((c.t, c.d), BF16),
+            pltpu.VMEM((2, c.cb, c.ff), F32),
+            dma((6,)),
         ],
         compiler_params=pltpu.CompilerParams(
             collective_id=0, has_side_effects=True, vmem_limit_bytes=60 * 2**20

time: 135 us -> 129 us (0.956)
  the two profiles are of different devices: /device:TPU:10 before, /device:TPU:1 now
where the time goes in v3:
time: 129 us
  Pallas kernels  122 us (95%)
  local copies, waits for them, and re-layouts  6.56 us (5%)
    pallas_call x1, Pallas kernels, local(): pl.pallas_call(functools.partial(kernel, c), out_shape=(jax.ShapeDtypeStr...  122 us
    unnamed x11, local copies, waits for them, and re-layouts  6.56 us

profile of v3, /device:TPU:1, one launch (start us, length us, event | category | flops | bytes accessed | tf_op | source)
XLA Modules:
  0.0 128.9 jit_solution(10511067225638666130)
XLA Ops:
  0.6 1.8 %copy.16 = bf16[128,2,768]{2,0,1:T(8,128)(2,1)} copy(bf16[128,2,768]{2,1,0:T(2,128)(2,1)} %param.13) | data formatting | bytes 786432 | tf_op args[3]
  2.4 121.7 %shard_map.129 = (bf16[128,4096]{1,0:T(8,128)(2,1)}, f32[128,2,768]{2,1,0:T(2,128)}, f32[16,4096]{1,0:T(8,128)}, f32[1,4096]{1,0:T(1,128)}) custom-call(bf16[128,4096]{1,0:T(8,128)(2,1)} %residual_hbm.1, f32[1,4096]{1,0:T(1,128)} %bitcast.10, bf16[16,4096]{1,0:T(8,128)(2,1)} %router_weight.1, bf16[2,128,768]{2,1,0:T(8,128)(2,1)} %bitcast.8, ...), custom_call_target="tpu_custom_call" | custom-call | flops 6039797760 | bytes 8388608 | tf_op jit(solution)/shard_map/pallas_call | solution.py:666
  124.1 0.0 copy-start
  124.1 2.4 %copy.21 = bf16[128,4096]{1,0:T(8,128)(2,1)} copy(bf16[128,4096]{1,0:T(8,128)(2,1)} %get-tuple-element.16) | data formatting | bytes 2097152
  126.5 0.0 copy-done
  126.5 0.0 copy-start.1
  126.5 0.9 copy.22
  127.4 0.2 copy-done.1
  127.6 0.0 copy-start.2
  127.6 0.7 copy.23
  128.3 0.0 copy-done.2
  128.3 0.6 copy.24
Async XLA Ops:
  124.1 2.4 %copy-start = (f32[128,2,768]{2,1,0:T(2,128)S(1)}, f32[128,2,768]{2,1,0:T(2,128)}, u32[]{:S(2)}) copy-start(f32[128,2,768]{2,1,0:T(2,128)} %get-tuple-element.17) | copy-start | bytes 2359300
  126.5 1.1 copy-start.1
  127.6 0.7 copy-start.2

commit v4 on v3

--- a/solution.py
+++ b/solution.py
@@ -105,6 +105,7 @@
     grad_hidden,
     residual,
     wg_own,
+    weight,
     sem_local,
 ):
     nz, nx, t, q, cb, cap, rows, m, blk = c.nz, c.nx, c.t, c.q, c.cb, c.cap, c.rows, c.m, c.blk
@@ -146,9 +147,8 @@
         )
 
     early = [
-        pltpu.make_async_copy(weight_hbm.at[0], wfull.at[0, z], sem_local.at[3]),
-        pltpu.make_async_copy(weight_hbm.at[1], wfull.at[1, z], sem_local.at[4]),
-        pltpu.make_async_copy(residual_hbm, residual, sem_local.at[5]),
+        pltpu.make_async_copy(residual_hbm, residual, sem_local.at[4]),
+        pltpu.make_async_copy(weight_hbm, weight, sem_local.at[3]),
     ]
     for copy in early:
         copy.start()
@@ -187,12 +187,6 @@
                 w_copy(i, way, s, piece).start()
 
     early[0].wait()
-    w_step(0, 1, 0)
-    w_step(0, 1, 1)
-    early[1].wait()
-    early[2].wait()
-    for copy in late:
-        copy.start()
 
     sums = jnp.zeros((t, cb), F32)
     for b in range(nz * NY):
@@ -213,10 +207,18 @@
     for d in (2, 1, 3):
         norm_slice(0, at_y(d))
         tok_copy(0, d).start()
+    early[1].wait()
+    for i in range(2):
+        wfull[i, z] = weight[:, i, :]
+        if i == 0:
+            w_step(0, 1, 0)
+            w_step(0, 1, 1)
+    for copy in late:
+        copy.start()
     norm_slice(0, y)
-    w_step(0, 2, 0)
     for p in range(NY):
         norm_slice(1, p)
+    w_step(0, 2, 0)
     for b in range(nz * NY):
         inner = slice((b // NY) * cb, (b // NY + 1) * cb)
         rw_slices[b % NY, :, inner] = router_weight[:, b * cb : (b + 1) * cb]
@@ -339,23 +341,20 @@
         for way in range(2):
             w_recv(i, way, half, way)
 
-        def wait_slots(d, carry):
-            for h in range(2):
-                ref = slots.at[i, h, at_x(nx - d)]
-                remote(ref, ref, sem_slot, (i, h, d - 1), to_x(nx - d)).wait_recv()
-            return carry
-
-        lax.fori_loop(1, nx, wait_slots, 0)
-
-        def step(h, carry):
+        chips = nx // 2
+        for back in [k for k in range(1, chips) if k < chips - 1] + [0, chips - 1]:
+            chip = (me // 2 - back + chips) % chips
+            for core in range(2) if back else range(1):
+                sender = chip * 2 + (core if back else 1 - me % 2)
+                gap = (me - sender + nx) % nx
+                for side in range(2):
+                    ref = slots.at[i, side, sender]
+                    remote(ref, ref, sem_slot, (i, side, gap - 1), {"expert": sender}).wait_recv()
             total = jnp.zeros((2 * rows, c.ff), F32)
             for side in range(2):
-                some = slots[i, side, pl.ds(2 * h, 2)].reshape(2 * rows, hq)
+                some = slots[i, side, pl.ds(2 * chip, 2)].reshape(2 * rows, hq)
                 total = total + nn(some, wfull[i, side * hz : (side + 1) * hz].reshape(hq, c.ff))
-            part[i, pl.ds(pl.multiple_of(h * 2 * rows, 16), 2 * rows), :] = total.astype(BF16)
-            return carry
-
-        lax.fori_loop(0, nx // 2, step, 0)
+            part[i, pl.ds(pl.multiple_of(chip * 2 * rows, 16), 2 * rows), :] = total.astype(BF16)
         part_perm[i, at_y(2)] = permuted(i, at_y(2)).astype(BF16)
         for way in range(2):
             rs_copy(i, way, 0).start()
@@ -466,7 +465,7 @@
                 terms = out.astype(F32) * slots[i, h, :, :, span].reshape(m, wide).astype(F32)
                 where = slice(h * hq + b * wide, h * hq + (b + 1) * wide)
                 gain_acc[:, where] += jnp.sum(terms.reshape(m // 8, 8, wide), axis=0)
-            if i == 0:
+            if i == 0 or h == 0:
                 send_backs(i, h)
             if h == 0:
                 wg_step(i, 1)
@@ -488,20 +487,21 @@
         lax.fori_loop(1, nx, wait_backs, 0)
         got = returned[i, h].reshape(m, hq)
         span = slice(h * hq, (h + 1) * hq)
-        for j in range(NY):
-            there = place[i, :, :, j * t : (j + 1) * t].reshape(m, t)
+        for d in (2, 1, 3, 0):
+            j = at_y(d)
+            there = place[i, :, :, pl.ds(pl.multiple_of(j * t, t), t)].reshape(m, t)
             if i == 0:
                 acc[j, :, span] = tn(there, got)
             else:
-                tok_back[h, j] = (acc[j, :, span] + tn(there, got)).astype(BF16)
+                total = (acc[j, :, span] + tn(there, got)).astype(BF16)
+                if d == 0:
+                    tok_ret[h, j] = total
+                else:
+                    tok_back[h, j] = total
+                    ret_copy(h, d).start()
 
     def ret_copy(h, d):
         return remote(tok_back.at[h, at_y(d)], tok_ret.at[h, y], sem_ret, (h, d - 1), to_y(d))
-
-    def send_ret(h):
-        for d in (2, 1, 3):
-            ret_copy(h, d).start()
-        tok_ret[h, y] = tok_back[h, y]
 
     def ar0_slice(e):
         return ar0.at[:, pl.ds(pl.multiple_of(e * cb, cb), cb)]
@@ -539,41 +539,38 @@
     ar0[c.e : c.e + 8, :] = gain_acc[...]
     for d in range(1, nx):
         ar_x(d).start()
-    send_backs(1, 0)
     send_backs(1, 1)
     ar1[me] = ar0[:, pl.ds(pl.multiple_of(me * cb, cb), cb)]
     for s in range(4, half + 1):
         wg_step(0, s)
     for h in range(2):
         combine(0, h)
+    wg_step(1, 2)
+    combine(1, 0)
     for d in range(1, nx):
         wait_ar((0, d - 1), ar1.at[at_x(nx - d)], to_x(nx - d))
     ar2[z] = jnp.sum(ar1[...], axis=0)
     for d in range(1, nz):
         ar_z(d).start()
-    wg_step(1, 2)
+    wg_step(1, 3)
     for d in range(1, nz):
         wait_ar((1, d - 1), ar2.at[at_z(-d)], to_z(-d))
     ar3[y] = jnp.sum(ar2[...], axis=0)
     for d in range(1, NY):
         ar_y(d).start()
-    combine(1, 0)
-    send_ret(0)
-    wg_step(1, 3)
+    for i in range(2):
+        wg_own[i] = weight_grad(i, z)
     for d in range(1, NY):
         wait_ar((2, d - 1), ar3.at[at_y(NY - d)], to_y(NY - d))
     ar4[me] = ar3[...]
     for d in range(1, nx):
         ar_out(d).start()
-    for i in range(2):
-        wg_own[i] = weight_grad(i, z)
     for s in range(4, half + 1):
         wg_step(1, s)
     for way in range(2):
         wg_recv(0, way, half)
     up_out[:, 0, :] = wg_own[0] + wg_in[0, 0, half - 1].astype(F32) + wg_in[0, 1, half - 1].astype(F32)
     combine(1, 1)
-    send_ret(1)
 
     for d in range(1, nx):
         wait_ar((3, d - 1), ar4.at[at_x(nx - d)], to_x(nx - d))
@@ -717,7 +714,8 @@
             pltpu.VMEM((2, c.blk, c.ff), BF16),
             pltpu.VMEM((c.t, c.d), BF16),
             pltpu.VMEM((2, c.cb, c.ff), F32),
-            dma((6,)),
+            pltpu.VMEM((c.cb, 2, c.ff), BF16),
+            dma((5,)),
         ],
         compiler_params=pltpu.CompilerParams(
             collective_id=0, has_side_effects=True, vmem_limit_bytes=60 * 2**20
@@ -729,7 +727,7 @@
         residual,
         norm_gain.reshape(1, c.d),
         router_weight,
-        up_weight.transpose(1, 0, 2),
+        up_weight,
         routes.T,
         keep_flags.T,
         gate_grad.T,

time: 129 us -> 128 us (level)
  local copies, waits for them, and re-layouts: 6.56 us -> 4.78 us
    unnamed x11 -> x10, local copies, waits for them, and re-layouts: 6.56 us -> 4.78 us
where the time goes in v4:
time: 128 us; the launch traced here: 127 us
  Pallas kernels  122 us (95%)
  local copies, waits for them, and re-layouts  4.78 us (4%)
    pallas_call x1, Pallas kernels, local(): pl.pallas_call(functools.partial(kernel, c), out_shape=(jax.ShapeDtypeStr...  122 us
    unnamed x10, local copies, waits for them, and re-layouts  4.78 us

profile of v4, /device:TPU:1, one launch (start us, length us, event | category | flops | bytes accessed | tf_op | source)
XLA Modules:
  0.0 127.1 jit_solution(6236905442790695455)
XLA Ops:
  0.6 121.7 %shard_map.129 = (bf16[128,4096]{1,0:T(8,128)(2,1)}, f32[128,2,768]{2,1,0:T(2,128)}, f32[16,4096]{1,0:T(8,128)}, f32[1,4096]{1,0:T(1,128)}) custom-call(bf16[128,4096]{1,0:T(8,128)(2,1)} %residual_hbm.1, f32[1,4096]{1,0:T(1,128)} %bitcast.6, bf16[16,4096]{1,0:T(8,128)(2,1)} %router_weight.1, bf16[128,2,768]{2,1,0:T(2,128)(2,1)} %weight_hbm.1, ...), custom_call_target="tpu_custom_call" | custom-call | flops 6039797760 | bytes 8388608 | tf_op jit(solution)/shard_map/pallas_call | solution.py:663
  122.3 0.0 copy-start
  122.4 2.4 %copy.18 = bf16[128,4096]{1,0:T(8,128)(2,1)} copy(bf16[128,4096]{1,0:T(8,128)(2,1)} %get-tuple-element.16) | data formatting | bytes 2097152
  124.7 0.0 copy-done
  124.7 0.0 copy-start.1
  124.7 0.9 copy.19
  125.6 0.2 copy-done.1
  125.8 0.0 copy-start.2
  125.8 0.7 copy.20
  126.5 0.0 copy-done.2
  126.5 0.6 copy.21
Async XLA Ops:
  122.3 2.4 %copy-start = (f32[128,2,768]{2,1,0:T(2,128)S(1)}, f32[128,2,768]{2,1,0:T(2,128)}, u32[]{:S(2)}) copy-start(f32[128,2,768]{2,1,0:T(2,128)} %get-tuple-element.17) | copy-start | bytes 2359300
  124.7 1.1 copy-start.1
  125.8 0.7 copy-start.2
